TPU v7x, 256 devices: a whole 4x4x8 slice. The times are simulated.
256 devices in a mesh: tm: 16 (over y, z_lo), row: 4 (over x), col: 4 (over z_hi, core).
Axes of the slice: x: 4, y: 4, z: 8 (z_hi: 2, z_lo: 4; z = z_hi * 4 + z_lo), core: 2. Of those that a mesh axis runs over, the one named last changes fastest.
Arguments:
- frame_features: bfloat16 [64, 16, 512, 128], P('tm', 'row', 'col'), may hold values from -6 to 6
- key_features: bfloat16 [16, 16, 512, 128], P('tm', 'row', 'col'), may hold values from -6 to 6
- key_index: int32 [64, 1], P('tm'), may hold values from 0 to 15, as said below
- motion_weight: bfloat16 [81, 128], replicated, may hold values from -0.625 to 0.625
- joint_weight: bfloat16 [3, 3, 256, 128], replicated, may hold values from -0.125 to 0.125
- dilated_weight: bfloat16 [3, 3, 128, 128], replicated, may hold values from -0.1875 to 0.1875
- flow_weight: bfloat16 [2, 3, 3, 128], replicated, may hold values from -0.1875 to 0.1875
Outputs:
- flow_update: float32 [64, 2, 16, 512], P('tm', None, 'row', 'col')
Inputs may be any that keep to these rules, and one draw needn't show every extreme that they name: `key_index`: frames come in blocks of 4 in order, block b holding frames b * 4 to (b + 1) * 4 - 1; a frame of block b names group b or group b - 1 (block 0 names only group 0); within a block the frames that name b - 1 come first; in every block b of 1 or more the first frame names b - 1, and the last frame of every block names b.
All inputs are finite; a program needn't handle non-finite values.
Results may differ from a plain program's by a relative error of at most 0.0048.
Values may be sent and summed in bfloat16 or wider, within the bound.
A program may use at most 64 MiB of HBM per device.

v0:
```python
import math

import jax
import jax.numpy as jnp
from jax import lax
from jax.sharding import PartitionSpec as P

RAD = 4


def extended(cells, sides, width):
    for axis, dim in sides:
        count = lax.axis_size(axis)
        ends = count - 1
        head = lax.slice_in_dim(cells, 0, width, axis=dim)
        tail = lax.slice_in_dim(cells, cells.shape[dim] - width, cells.shape[dim], axis=dim)
        cells = jnp.concatenate(
            [
                lax.ppermute(tail, axis, [(i, (i + 1) % count) for i in range(ends)]),
                cells,
                lax.ppermute(head, axis, [((i + 1) % count, i) for i in range(ends)]),
            ],
            axis=dim,
        )
    return cells


def passed_along(array, axis, by):
    count = lax.axis_size(axis)
    pairs = [(i, i + by) for i in range(count) if 0 <= i + by < count]
    return lax.ppermute(array, axis, pairs)


def convolve(source, weight, spread):
    out_rows = source.shape[1] - 2 * spread
    out_columns = source.shape[2] - 2 * spread
    totals = jnp.zeros((source.shape[0], out_rows, out_columns, weight.shape[3]), jnp.float32)
    for tap_row in range(3):
        for tap_column in range(3):
            window = source[
                :,
                tap_row * spread : tap_row * spread + out_rows,
                tap_column * spread : tap_column * spread + out_columns,
                :,
            ]
            totals = totals + jnp.einsum(
                "fyxc,ck->fyxk",
                window,
                weight[tap_row, tap_column],
                preferred_element_type=jnp.float32,
            )
    return totals


def flow_head(source, flow_weight):
    out_rows = source.shape[1] - 2
    out_columns = source.shape[2] - 2
    totals = jnp.zeros((source.shape[0], flow_weight.shape[0], out_rows, out_columns), jnp.float32)
    for tap_row in range(3):
        for tap_column in range(3):
            window = source[
                :, tap_row : tap_row + out_rows, tap_column : tap_column + out_columns, :
            ]
            totals = totals + jnp.einsum(
                "fyxc,kc->fkyx",
                window,
                flow_weight[:, tap_row, tap_column, :],
                preferred_element_type=jnp.float32,
            )
    return totals


def correlate(queries, keyframes, motion_weight):
    frames, tile_rows, tile_columns, channels = queries.shape
    window_size = 2 * RAD + 1
    scaling = 1.0 / math.sqrt(channels)
    padded_rows = tile_rows + 2 * RAD
    totals = jnp.zeros((frames, tile_rows, tile_columns, motion_weight.shape[1]), jnp.float32)
    for shift_column in range(window_size):
        window = keyframes[:, :, shift_column : shift_column + tile_columns, :]
        scores = jnp.einsum("fyxc,fvxc->fyvx", queries, window, preferred_element_type=jnp.float32)
        flattened = scores.reshape(frames, tile_rows * padded_rows, tile_columns)
        flattened = jnp.pad(flattened, ((0, 0), (0, tile_rows), (0, 0)))
        banded = flattened.reshape(frames, tile_rows, padded_rows + 1, tile_columns)[
            :, :, :window_size, :
        ]
        rounded = (banded * scaling).astype(jnp.bfloat16)
        weight_rows = motion_weight[shift_column::window_size]
        totals = totals + jnp.einsum(
            "fydx,dk->fyxk", rounded, weight_rows, preferred_element_type=jnp.float32
        )
    return jax.nn.relu(totals).astype(jnp.bfloat16)


def local(
    frame_features,
    key_features,
    key_index,
    motion_weight,
    joint_weight,
    dilated_weight,
    flow_weight,
):
    chosen_groups = key_index[:, 0]
    widened = extended(key_features, (("row", 1), ("col", 2)), RAD)
    previous = passed_along(widened, "tm", 1)
    paired = jnp.concatenate([previous, widened], axis=0)
    local_groups = chosen_groups - lax.axis_index("tm") + 1
    keyframes = jnp.take(paired, local_groups, axis=0)
    motion = correlate(frame_features, keyframes, motion_weight)
    joined = jnp.concatenate([motion, frame_features], axis=3)
    border_joint = extended(joined, (("row", 1), ("col", 2)), 1)
    hidden_one = jax.nn.relu(convolve(border_joint, joint_weight, 1)).astype(jnp.bfloat16)
    border_one = extended(hidden_one, (("row", 1), ("col", 2)), 2)
    hidden_two = jax.nn.relu(convolve(border_one, dilated_weight, 2)).astype(jnp.bfloat16)
    border_two = extended(hidden_two, (("row", 1), ("col", 2)), 1)
    return flow_head(border_two, flow_weight)


def solution(mesh):
    in_specs = (
        P("tm", "row", "col", None),
        P("tm", "row", "col", None),
        P("tm", None),
        P(),
        P(),
        P(),
        P(),
    )
    out_specs = P("tm", None, "row", "col")
    return jax.shard_map(local, mesh=mesh, in_specs=in_specs, out_specs=out_specs, check_vma=False)
```

profile of v0, /device:TPU:1, one launch (start us, length us, event | category | flops | bytes accessed | tf_op | source)
XLA Modules:
  0.0 198.8 jit_solution(8031949716597248606)
XLA Ops:
  0.0 4.1 %collective-permute-start = (bf16[1,4,128,128]{3,2,1,0:T(8,128)(2,1)}, bf16[1,4,128,128]{3,2,1,0:T(8,128)(2,1)S(1)}, u32[]{:S(2)}, u32[]{:S(2)}) collective-permute-start(bf16[1,4,128,128]{3,2,1,0:T(8,128)(2,1)} %param.8), channel_id=1, source_target_pairs={{0,4},{4,8},{8,12},{1,5},{5,9},{9,13},{2,6},{6,10},{10,14},{3,7},{... | collective-permute-start | bytes 393224 | tf_op jit(solution)/shard_map/ppermute | solution.py:19
  7.5 2.5 %collective-permute-done.1 = bf16[1,4,128,128]{3,2,1,0:T(8,128)(2,1)S(1)} collective-permute-done((bf16[1,4,128,128]{3,2,1,0:T(8,128)(2,1)}, bf16[1,4,128,128]{3,2,1,0:T(8,128)(2,1)S(1)}, u32[]{:S(2)}, u32[]{:S(2)}) %collective-permute-start.1) | collective-permute-done | bytes 131104 | tf_op jit(solution)/shard_map/ppermute | solution.py:21
  10.1 10.8 %collective-permute-start.2 = (bf16[1,12,4,128]{3,2,1,0:T(4,128)(2,1)S(1)}, bf16[1,12,4,128]{3,2,1,0:T(4,128)(2,1)S(1)}, u32[]{:S(2)}, u32[]{:S(2)}) collective-permute-start(bf16[1,12,4,128]{3,2,1,0:T(4,128)(2,1)S(1)} %get-tuple-element.23), channel_id=1, source_target_pairs={{0,1},{1,2},{2,3},{4,5},{5,6},{6,7},{8,9},{9,10},{10,11},{12,13},{... | collective-permute-start | bytes 36872 | tf_op jit(solution)/shard_map/ppermute | solution.py:19
  22.8 7.2 %collective-permute-done.3 = bf16[1,12,4,128]{3,2,1,0:T(4,128)(2,1)S(1)} collective-permute-done((bf16[1,12,4,128]{3,2,1,0:T(4,128)(2,1)S(1)}, bf16[1,12,4,128]{3,2,1,0:T(4,128)(2,1)S(1)}, u32[]{:S(2)}, u32[]{:S(2)}) %collective-permute-start.3) | collective-permute-done | bytes 12320 | tf_op jit(solution)/shard_map/ppermute | solution.py:21
  30.1 2.5 %collective-permute-start.4 = (bf16[1,12,136,128]{3,2,1,0:T(8,128)(2,1)S(1)}, bf16[1,12,136,128]{3,2,1,0:T(8,128)(2,1)S(1)}, u32[]{:S(2)}, u32[]{:S(2)}) collective-permute-start(bf16[1,12,136,128]{3,2,1,0:T(8,128)(2,1)S(1)} %pad_maximum_fusion.17), channel_id=1, source_target_pairs={{0,16},{16,32},{32,48},{48,64},{64,80},{80,96},{96,112},{112,128},... | collective-permute-start | bytes 1253384 | tf_op jit(solution)/shard_map/ppermute | solution.py:31
  64.1 3.0 %convolution_bitcast_fusion.7 = f32[4,4,12,128]{2,1,3,0:T(4,128)S(1)} fusion(bf16[4,4,128,128]{3,2,1,0:T(8,128)(2,1)} %param.7, bf16[4,12,136,128]{3,1,2,0:T(8,128)(2,1)} %copy_select_fusion.35), kind=kOutput, calls=%fused_computation.41 | convolution fusion | flops 6291456 | bytes 2293760 | tf_op jit(solution)/shard_map/fyxc,fvxc->fyvx/dot_general | solution.py:81
  68.1 2.2 %convolution_bitcast_fusion.6 = f32[4,4,12,128]{2,1,3,0:T(4,128)S(1)} fusion(bf16[4,4,128,128]{3,2,1,0:T(8,128)(2,1)} %param.7, bf16[4,12,136,128]{3,1,2,0:T(8,128)(2,1)S(1)} %copy-done.10), kind=kOutput, calls=%fused_computation.40 | convolution fusion | flops 6291456 | bytes 2293760 | tf_op jit(solution)/shard_map/fyxc,fvxc->fyvx/dot_general | solution.py:81
  71.4 3.0 %convolution_bitcast_fusion.5 = f32[4,4,12,128]{2,1,3,0:T(4,128)S(1)} fusion(bf16[4,4,128,128]{3,2,1,0:T(8,128)(2,1)} %param.7, bf16[4,12,136,128]{3,1,2,0:T(8,128)(2,1)} %copy_select_fusion.33), kind=kOutput, calls=%fused_computation.39 | convolution fusion | flops 6291456 | bytes 2293760 | tf_op jit(solution)/shard_map/fyxc,fvxc->fyvx/dot_general | solution.py:81
  75.5 2.2 %convolution_bitcast_fusion.4 = f32[4,4,12,128]{2,1,3,0:T(4,128)S(1)} fusion(bf16[4,4,128,128]{3,2,1,0:T(8,128)(2,1)} %param.7, bf16[4,12,136,128]{3,1,2,0:T(8,128)(2,1)S(1)} %copy-done.9), kind=kOutput, calls=%fused_computation.38 | convolution fusion | flops 6291456 | bytes 2293760 | tf_op jit(solution)/shard_map/fyxc,fvxc->fyvx/dot_general | solution.py:81
  78.1 3.0 %convolution_bitcast_fusion.3 = f32[4,4,12,128]{2,1,3,0:T(4,128)S(1)} fusion(bf16[4,4,128,128]{3,2,1,0:T(8,128)(2,1)} %param.7, bf16[4,12,136,128]{3,1,2,0:T(8,128)(2,1)} %copy_select_fusion.31), kind=kOutput, calls=%fused_computation.37 | convolution fusion | flops 6291456 | bytes 2293760 | tf_op jit(solution)/shard_map/fyxc,fvxc->fyvx/dot_general | solution.py:81
  81.6 2.4 %convolution_bitcast_fusion.2 = f32[4,4,12,128]{2,1,3,0:T(4,128)S(1)} fusion(bf16[4,4,128,128]{3,2,1,0:T(8,128)(2,1)} %param.7, bf16[4,12,136,128]{3,1,2,0:T(8,128)(2,1)S(1)} %copy-done.8), kind=kOutput, calls=%fused_computation.36 | convolution fusion | flops 6291456 | bytes 2293760 | tf_op jit(solution)/shard_map/fyxc,fvxc->fyvx/dot_general | solution.py:81
  85.0 3.0 %convolution_bitcast_fusion.1 = f32[4,4,12,128]{2,1,3,0:T(4,128)S(1)} fusion(bf16[4,4,128,128]{3,2,1,0:T(8,128)(2,1)} %param.7, bf16[4,12,136,128]{3,1,2,0:T(8,128)(2,1)} %copy_select_fusion.29), kind=kOutput, calls=%fused_computation.35 | convolution fusion | flops 6291456 | bytes 2293760 | tf_op jit(solution)/shard_map/fyxc,fvxc->fyvx/dot_general | solution.py:81
  90.6 2.2 %convolution_bitcast_fusion = f32[4,4,12,128]{2,1,3,0:T(4,128)S(1)} fusion(bf16[4,4,128,128]{3,2,1,0:T(8,128)(2,1)} %param.7, bf16[4,12,136,128]{3,1,2,0:T(8,128)(2,1)S(1)} %copy-done.7), kind=kOutput, calls=%fused_computation.34 | convolution fusion | flops 6291456 | bytes 2293760 | tf_op jit(solution)/shard_map/fyxc,fvxc->fyvx/dot_general | solution.py:81
  97.3 3.1 %collective-permute-start.5 = (bf16[4,1,128,256]{2,3,1,0:T(8,128)(2,1)S(1)}, bf16[4,1,128,256]{2,3,1,0:T(8,128)(2,1)S(1)}, u32[]{:S(2)}, u32[]{:S(2)}) collective-permute-start(bf16[4,1,128,256]{2,3,1,0:T(8,128)(2,1)S(1)} %get-tuple-element.13), channel_id=1, source_target_pairs={{0,4},{4,8},{8,12},{1,5},{5,9},{9,13},{2,6},{6,10},{10,14},{3,7},{... | collective-permute-start | bytes 786440 | tf_op jit(solution)/shard_map/ppermute | solution.py:19
  104.0 3.6 %collective-permute-done.6 = bf16[4,1,128,256]{2,3,1,0:T(8,128)(2,1)S(1)} collective-permute-done((bf16[4,1,128,256]{2,3,1,0:T(8,128)(2,1)S(1)}, bf16[4,1,128,256]{2,3,1,0:T(8,128)(2,1)S(1)}, u32[]{:S(2)}, u32[]{:S(2)}) %collective-permute-start.6) | collective-permute-done | bytes 262176 | tf_op jit(solution)/shard_map/ppermute | solution.py:21
  111.3 3.6 %collective-permute-start.7 = (bf16[4,6,1,256]{3,0,2,1:T(4,128)(2,1)S(1)}, bf16[4,6,1,256]{3,0,2,1:T(4,128)(2,1)S(1)}, u32[]{:S(2)}, u32[]{:S(2)}) collective-permute-start(bf16[4,6,1,256]{3,0,2,1:T(4,128)(2,1)S(1)} %copy.177), channel_id=1, source_target_pairs={{0,1},{1,2},{2,3},{4,5},{5,6},{6,7},{8,9},{9,10},{10,11},{12,13},{... | collective-permute-start | bytes 36872 | tf_op jit(solution)/shard_map/ppermute | solution.py:19
  117.6 2.2 %fusion.15 = f32[4,4,128,128]{2,3,1,0:T(8,128)} fusion(bf16[4,4,128,128]{2,3,1,0:T(8,128)(2,1)S(1)} %copy-done, bf16[4,4,128,128]{2,3,1,0:T(8,128)(2,1)S(1)} %fusion.29, bf16[4,1,128,256]{2,3,1,0:T(8,128)(2,1)S(1)} %collective-permute-done.5, bf16[3,3,256,128]{3,2,1,0:T(8,128)(2,1)} %param.11), kind=kOutput, calls=%fused_computation.43 | convolution fusion | flops 138149888 | bytes 2424832 | tf_op jit(solution)/shard_map/fyxc,ck->fyxk/dot_general | solution.py:46
  126.1 4.4 %maximum_maximum_fusion = (bf16[4,6,129,256]{2,3,1,0:T(8,128)(2,1)S(1)}, bf16[4,6,129,256]{2,3,1,0:T(8,128)(2,1)S(1)}) fusion(bf16[4,1,128,256]{2,3,1,0:T(8,128)(2,1)S(1)} %collective-permute-done.6, bf16[4,4,128,128]{2,3,1,0:T(8,128)(2,1)S(1)} %copy-done, bf16[4,4,128,128]{2,3,1,0:T(8,128)(2,1)S(1)} %fusion.29, ...), kind=kLoop, calls=%fused_computation.1 | loop fusion | flops 15851520 | bytes 4767744 | tf_op jit(solution)/shard_map/concatenate | solution.py:17
  135.2 2.8 %collective-permute-start.9 = (bf16[4,2,128,128]{2,3,1,0:T(8,128)(2,1)S(1)}, bf16[4,2,128,128]{2,3,1,0:T(8,128)(2,1)S(1)}, u32[]{:S(2)}, u32[]{:S(2)}) collective-permute-start(bf16[4,2,128,128]{2,3,1,0:T(8,128)(2,1)S(1)} %get-tuple-element.21), channel_id=1, source_target_pairs={{0,4},{4,8},{8,12},{1,5},{5,9},{9,13},{2,6},{6,10},{10,14},{3,7},{... | collective-permute-start | bytes 786440 | tf_op jit(solution)/shard_map/ppermute | solution.py:19
  141.3 3.9 %collective-permute-done.10 = bf16[4,2,128,128]{2,3,1,0:T(8,128)(2,1)S(1)} collective-permute-done((bf16[4,2,128,128]{2,3,1,0:T(8,128)(2,1)S(1)}, bf16[4,2,128,128]{2,3,1,0:T(8,128)(2,1)S(1)}, u32[]{:S(2)}, u32[]{:S(2)}) %collective-permute-start.10) | collective-permute-done | bytes 262176 | tf_op jit(solution)/shard_map/ppermute | solution.py:21
  150.7 7.5 %collective-permute-start.11 = (bf16[4,8,2,128]{3,1,2,0:T(8,128)(2,1)S(1)}, bf16[4,8,2,128]{3,1,2,0:T(8,128)(2,1)S(1)}, u32[]{:S(2)}, u32[]{:S(2)}) collective-permute-start(bf16[4,8,2,128]{3,1,2,0:T(8,128)(2,1)S(1)} %copy.199), channel_id=1, source_target_pairs={{0,1},{1,2},{2,3},{4,5},{5,6},{6,7},{8,9},{9,10},{10,11},{12,13},{... | collective-permute-start | bytes 49160 | tf_op jit(solution)/shard_map/ppermute | solution.py:19
  173.3 3.8 %collective-permute-done.14 = bf16[4,1,128,128]{2,3,1,0:T(8,128)(2,1)S(1)} collective-permute-done((bf16[4,1,128,128]{2,3,1,0:T(8,128)(2,1)S(1)}, bf16[4,1,128,128]{2,3,1,0:T(8,128)(2,1)S(1)}, u32[]{:S(2)}, u32[]{:S(2)}) %collective-permute-start.14) | collective-permute-done | bytes 131104 | tf_op jit(solution)/shard_map/ppermute | solution.py:21
  177.8 7.7 %collective-permute-start.15 = (bf16[4,6,1,128]{3,0,2,1:T(4,128)(2,1)S(1)}, bf16[4,6,1,128]{3,0,2,1:T(4,128)(2,1)S(1)}, u32[]{:S(2)}, u32[]{:S(2)}) collective-permute-start(bf16[4,6,1,128]{3,0,2,1:T(4,128)(2,1)S(1)} %copy.221), channel_id=1, source_target_pairs={{0,1},{1,2},{2,3},{4,5},{5,6},{6,7},{8,9},{9,10},{10,11},{12,13},{... | collective-permute-start | bytes 18440 | tf_op jit(solution)/shard_map/ppermute | solution.py:19
  188.6 6.1 %collective-permute-done.16 = bf16[4,6,1,128]{3,0,2,1:T(4,128)(2,1)S(1)} collective-permute-done((bf16[4,6,1,128]{3,0,2,1:T(4,128)(2,1)S(1)}, bf16[4,6,1,128]{3,0,2,1:T(4,128)(2,1)S(1)}, u32[]{:S(2)}, u32[]{:S(2)}) %collective-permute-start.16) | collective-permute-done | bytes 6176 | tf_op jit(solution)/shard_map/ppermute | solution.py:21
  (200 shorter events, 101.0 us)
Async XLA Ops:
  0.0 46.7 %copy-start.31 = (s32[4,1]{0,1:T(1,128)S(1)}, s32[4,1]{0,1:T(1,128)}, u32[]{:S(2)}) copy-start(s32[4,1]{0,1:T(1,128)} %param.9) | copy-start | bytes 52
  0.0 6.5 %collective-permute-start = (bf16[1,4,128,128]{3,2,1,0:T(8,128)(2,1)}, bf16[1,4,128,128]{3,2,1,0:T(8,128)(2,1)S(1)}, u32[]{:S(2)}, u32[]{:S(2)}) collective-permute-start(bf16[1,4,128,128]{3,2,1,0:T(8,128)(2,1)} %param.8), channel_id=1, source_target_pairs={{0,4},{4,8},{8,12},{1,5},{5,9},{9,13},{2,6},{6,10},{10,14},{3,7},{... | collective-permute-start | bytes 393224 | tf_op jit(solution)/shard_map/ppermute | solution.py:19
  4.1 5.9 %collective-permute-start.1 = (bf16[1,4,128,128]{3,2,1,0:T(8,128)(2,1)}, bf16[1,4,128,128]{3,2,1,0:T(8,128)(2,1)S(1)}, u32[]{:S(2)}, u32[]{:S(2)}) collective-permute-start(bf16[1,4,128,128]{3,2,1,0:T(8,128)(2,1)} %param.8), channel_id=1, source_target_pairs={{4,0},{8,4},{12,8},{5,1},{9,5},{13,9},{6,2},{10,6},{14,10},{7,3},{... | collective-permute-start | bytes 393224 | tf_op jit(solution)/shard_map/ppermute | solution.py:21
  10.1 12.7 %collective-permute-start.2 = (bf16[1,12,4,128]{3,2,1,0:T(4,128)(2,1)S(1)}, bf16[1,12,4,128]{3,2,1,0:T(4,128)(2,1)S(1)}, u32[]{:S(2)}, u32[]{:S(2)}) collective-permute-start(bf16[1,12,4,128]{3,2,1,0:T(4,128)(2,1)S(1)} %get-tuple-element.23), channel_id=1, source_target_pairs={{0,1},{1,2},{2,3},{4,5},{5,6},{6,7},{8,9},{9,10},{10,11},{12,13},{... | collective-permute-start | bytes 36872 | tf_op jit(solution)/shard_map/ppermute | solution.py:19
  20.9 9.1 %collective-permute-start.3 = (bf16[1,12,4,128]{3,2,1,0:T(4,128)(2,1)S(1)}, bf16[1,12,4,128]{3,2,1,0:T(4,128)(2,1)S(1)}, u32[]{:S(2)}, u32[]{:S(2)}) collective-permute-start(bf16[1,12,4,128]{3,2,1,0:T(4,128)(2,1)S(1)} %get-tuple-element.24), channel_id=1, source_target_pairs={{1,0},{2,1},{3,2},{5,4},{6,5},{7,6},{9,8},{10,9},{11,10},{13,12},{... | collective-permute-start | bytes 36872 | tf_op jit(solution)/shard_map/ppermute | solution.py:21
  30.1 16.6 %collective-permute-start.4 = (bf16[1,12,136,128]{3,2,1,0:T(8,128)(2,1)S(1)}, bf16[1,12,136,128]{3,2,1,0:T(8,128)(2,1)S(1)}, u32[]{:S(2)}, u32[]{:S(2)}) collective-permute-start(bf16[1,12,136,128]{3,2,1,0:T(8,128)(2,1)S(1)} %pad_maximum_fusion.17), channel_id=1, source_target_pairs={{0,16},{16,32},{32,48},{48,64},{64,80},{80,96},{96,112},{112,128},... | collective-permute-start | bytes 1253384 | tf_op jit(solution)/shard_map/ppermute | solution.py:31
  64.1 4.0 %copy-start.10 = (bf16[4,12,136,128]{3,1,2,0:T(8,128)(2,1)S(1)}, bf16[4,12,136,128]{3,1,2,0:T(8,128)(2,1)}, u32[]{:S(2)}) copy-start(bf16[4,12,136,128]{3,1,2,0:T(8,128)(2,1)} %copy_select_fusion.34) | copy-start | bytes 5013508
  71.4 4.1 %copy-start.9 = (bf16[4,12,136,128]{3,1,2,0:T(8,128)(2,1)S(1)}, bf16[4,12,136,128]{3,1,2,0:T(8,128)(2,1)}, u32[]{:S(2)}) copy-start(bf16[4,12,136,128]{3,1,2,0:T(8,128)(2,1)} %copy_select_fusion.32) | copy-start | bytes 5013508
  85.0 5.6 %copy-start.7 = (bf16[4,12,136,128]{3,1,2,0:T(8,128)(2,1)S(1)}, bf16[4,12,136,128]{3,1,2,0:T(8,128)(2,1)}, u32[]{:S(2)}) copy-start(bf16[4,12,136,128]{3,1,2,0:T(8,128)(2,1)} %copy_select_fusion.28) | copy-start | bytes 5013508
  97.3 6.6 %collective-permute-start.5 = (bf16[4,1,128,256]{2,3,1,0:T(8,128)(2,1)S(1)}, bf16[4,1,128,256]{2,3,1,0:T(8,128)(2,1)S(1)}, u32[]{:S(2)}, u32[]{:S(2)}) collective-permute-start(bf16[4,1,128,256]{2,3,1,0:T(8,128)(2,1)S(1)} %get-tuple-element.13), channel_id=1, source_target_pairs={{0,4},{4,8},{8,12},{1,5},{5,9},{9,13},{2,6},{6,10},{10,14},{3,7},{... | collective-permute-start | bytes 786440 | tf_op jit(solution)/shard_map/ppermute | solution.py:19
  100.5 7.1 %collective-permute-start.6 = (bf16[4,1,128,256]{2,3,1,0:T(8,128)(2,1)S(1)}, bf16[4,1,128,256]{2,3,1,0:T(8,128)(2,1)S(1)}, u32[]{:S(2)}, u32[]{:S(2)}) collective-permute-start(bf16[4,1,128,256]{2,3,1,0:T(8,128)(2,1)S(1)} %get-tuple-element.14), channel_id=1, source_target_pairs={{4,0},{8,4},{12,8},{5,1},{9,5},{13,9},{6,2},{10,6},{14,10},{7,3},{... | collective-permute-start | bytes 786440 | tf_op jit(solution)/shard_map/ppermute | solution.py:21
  111.3 10.7 %collective-permute-start.7 = (bf16[4,6,1,256]{3,0,2,1:T(4,128)(2,1)S(1)}, bf16[4,6,1,256]{3,0,2,1:T(4,128)(2,1)S(1)}, u32[]{:S(2)}, u32[]{:S(2)}) collective-permute-start(bf16[4,6,1,256]{3,0,2,1:T(4,128)(2,1)S(1)} %copy.177), channel_id=1, source_target_pairs={{0,1},{1,2},{2,3},{4,5},{5,6},{6,7},{8,9},{9,10},{10,11},{12,13},{... | collective-permute-start | bytes 36872 | tf_op jit(solution)/shard_map/ppermute | solution.py:19
  115.6 8.9 %collective-permute-start.8 = (bf16[4,6,1,256]{3,0,2,1:T(4,128)(2,1)S(1)}, bf16[4,6,1,256]{3,0,2,1:T(4,128)(2,1)S(1)}, u32[]{:S(2)}, u32[]{:S(2)}) collective-permute-start(bf16[4,6,1,256]{3,0,2,1:T(4,128)(2,1)S(1)} %copy.183), channel_id=1, source_target_pairs={{1,0},{2,1},{3,2},{5,4},{6,5},{7,6},{9,8},{10,9},{11,10},{13,12},{... | collective-permute-start | bytes 36872 | tf_op jit(solution)/shard_map/ppermute | solution.py:21
  126.1 4.4 %copy-start.20 = (bf16[3,3,256,128]{3,2,1,0:T(8,128)(2,1)S(1)}, bf16[3,3,256,128]{3,2,1,0:T(8,128)(2,1)}, u32[]{:S(2)}) copy-start(bf16[3,3,256,128]{3,2,1,0:T(8,128)(2,1)} %param.11) | copy-start | bytes 1769476
  134.5 5.1 %copy-start.21 = (bf16[3,3,128,128]{3,2,1,0:T(8,128)(2,1)S(1)}, bf16[3,3,128,128]{3,2,1,0:T(8,128)(2,1)}, u32[]{:S(2)}) copy-start(bf16[3,3,128,128]{3,2,1,0:T(8,128)(2,1)} %param.12) | copy-start | bytes 884740
  135.2 6.1 %collective-permute-start.9 = (bf16[4,2,128,128]{2,3,1,0:T(8,128)(2,1)S(1)}, bf16[4,2,128,128]{2,3,1,0:T(8,128)(2,1)S(1)}, u32[]{:S(2)}, u32[]{:S(2)}) collective-permute-start(bf16[4,2,128,128]{2,3,1,0:T(8,128)(2,1)S(1)} %get-tuple-element.21), channel_id=1, source_target_pairs={{0,4},{4,8},{8,12},{1,5},{5,9},{9,13},{2,6},{6,10},{10,14},{3,7},{... | collective-permute-start | bytes 786440 | tf_op jit(solution)/shard_map/ppermute | solution.py:19
  138.1 7.2 %collective-permute-start.10 = (bf16[4,2,128,128]{2,3,1,0:T(8,128)(2,1)S(1)}, bf16[4,2,128,128]{2,3,1,0:T(8,128)(2,1)S(1)}, u32[]{:S(2)}, u32[]{:S(2)}) collective-permute-start(bf16[4,2,128,128]{2,3,1,0:T(8,128)(2,1)S(1)} %get-tuple-element.22), channel_id=1, source_target_pairs={{4,0},{8,4},{12,8},{5,1},{9,5},{13,9},{6,2},{10,6},{14,10},{7,3},{... | collective-permute-start | bytes 786440 | tf_op jit(solution)/shard_map/ppermute | solution.py:21
  148.4 15.9 %collective-permute-start.12 = (bf16[4,8,2,128]{3,1,2,0:T(8,128)(2,1)S(1)}, bf16[4,8,2,128]{3,1,2,0:T(8,128)(2,1)S(1)}, u32[]{:S(2)}, u32[]{:S(2)}) collective-permute-start(bf16[4,8,2,128]{3,1,2,0:T(8,128)(2,1)S(1)} %copy.205), channel_id=1, source_target_pairs={{1,0},{2,1},{3,2},{5,4},{6,5},{7,6},{9,8},{10,9},{11,10},{13,12},{... | collective-permute-start | bytes 49160 | tf_op jit(solution)/shard_map/ppermute | solution.py:21
  150.7 10.2 %collective-permute-start.11 = (bf16[4,8,2,128]{3,1,2,0:T(8,128)(2,1)S(1)}, bf16[4,8,2,128]{3,1,2,0:T(8,128)(2,1)S(1)}, u32[]{:S(2)}, u32[]{:S(2)}) collective-permute-start(bf16[4,8,2,128]{3,1,2,0:T(8,128)(2,1)S(1)} %copy.199), channel_id=1, source_target_pairs={{0,1},{1,2},{2,3},{4,5},{5,6},{6,7},{8,9},{9,10},{10,11},{12,13},{... | collective-permute-start | bytes 49160 | tf_op jit(solution)/shard_map/ppermute | solution.py:19
  168.8 3.9 %copy-start.32 = (bf16[2,3,3,128]{3,0,2,1:T(2,128)(2,1)S(1)}, bf16[2,3,3,128]{3,0,2,1:T(2,128)(2,1)}, u32[]{:S(2)}) copy-start(bf16[2,3,3,128]{3,0,2,1:T(2,128)(2,1)} %param.13) | copy-start | bytes 13828
  169.4 3.8 %collective-permute-start.13 = (bf16[4,1,128,128]{2,3,1,0:T(8,128)(2,1)S(1)}, bf16[4,1,128,128]{2,3,1,0:T(8,128)(2,1)S(1)}, u32[]{:S(2)}, u32[]{:S(2)}) collective-permute-start(bf16[4,1,128,128]{2,3,1,0:T(8,128)(2,1)S(1)} %get-tuple-element.19), channel_id=1, source_target_pairs={{0,4},{4,8},{8,12},{1,5},{5,9},{9,13},{2,6},{6,10},{10,14},{3,7},{... | collective-permute-start | bytes 393224 | tf_op jit(solution)/shard_map/ppermute | solution.py:19
  171.3 5.7 %collective-permute-start.14 = (bf16[4,1,128,128]{2,3,1,0:T(8,128)(2,1)S(1)}, bf16[4,1,128,128]{2,3,1,0:T(8,128)(2,1)S(1)}, u32[]{:S(2)}, u32[]{:S(2)}) collective-permute-start(bf16[4,1,128,128]{2,3,1,0:T(8,128)(2,1)S(1)} %get-tuple-element.20), channel_id=1, source_target_pairs={{4,0},{8,4},{12,8},{5,1},{9,5},{13,9},{6,2},{10,6},{14,10},{7,3},{... | collective-permute-start | bytes 393224 | tf_op jit(solution)/shard_map/ppermute | solution.py:21
  177.8 10.3 %collective-permute-start.15 = (bf16[4,6,1,128]{3,0,2,1:T(4,128)(2,1)S(1)}, bf16[4,6,1,128]{3,0,2,1:T(4,128)(2,1)S(1)}, u32[]{:S(2)}, u32[]{:S(2)}) collective-permute-start(bf16[4,6,1,128]{3,0,2,1:T(4,128)(2,1)S(1)} %copy.221), channel_id=1, source_target_pairs={{0,1},{1,2},{2,3},{4,5},{5,6},{6,7},{8,9},{9,10},{10,11},{12,13},{... | collective-permute-start | bytes 18440 | tf_op jit(solution)/shard_map/ppermute | solution.py:19
  185.9 8.9 %collective-permute-start.16 = (bf16[4,6,1,128]{3,0,2,1:T(4,128)(2,1)S(1)}, bf16[4,6,1,128]{3,0,2,1:T(4,128)(2,1)S(1)}, u32[]{:S(2)}, u32[]{:S(2)}) collective-permute-start(bf16[4,6,1,128]{3,0,2,1:T(4,128)(2,1)S(1)} %copy.225), channel_id=1, source_target_pairs={{1,0},{2,1},{3,2},{5,4},{6,5},{7,6},{9,8},{10,9},{11,10},{13,12},{... | collective-permute-start | bytes 18440 | tf_op jit(solution)/shard_map/ppermute | solution.py:21
  (26 other events, 34.9 us)
where the time goes:
time: 201 us; the launch traced here: 199 us
  starting transfers between devices  57.2 us (28%)
  matrix products  45.8 us (23%)
  local copies, waits for them, and re-layouts  43.6 us (22%)
  waiting for transfers between devices  30.8 us (15%)
  other arithmetic  20.7 us (10%)
    ppermute x8, starting transfers between devices, extended(): lax.ppermute(tail, axis, [(i, (i + 1) % count) for i in range(ends)])  41.7 us
    ppermute x8, waiting for transfers between devices, extended(): lax.ppermute(head, axis, [((i + 1) % count, i) for i in range(ends)])  28.8 us
    dot_general x9, matrix products, correlate(): jnp.einsum('fyxc,fvxc->fyvx', queries, window, preferred_element_type=jnp...  22.2 us
    dot_general x18, matrix products, convolve(): jnp.einsum('fyxc,ck->fyxk', window, weight[tap_row, tap_column], preferre...  18.5 us
    dot_general x9, other arithmetic, correlate(): jnp.einsum('fyxc,fvxc->fyvx', queries, window, preferred_element_type=jnp...  14.1 us
    ppermute x8, starting transfers between devices, extended(): lax.ppermute(head, axis, [((i + 1) % count, i) for i in range(ends)])  13.1 us
    slice x9, local copies, waits for them, and re-layouts, correlate(): weight_rows = motion_weight[shift_column::window_size]  12 us
    unnamed x69, local copies, waits for them, and re-layouts  7.85 us
  transfers between devices with their start and end apart: 17, of which 10 were waited for; matrix products, arithmetic and copies ran while one was open for 16% of the time, Pallas kernels for 0%

commit v1 on v0

v1 whole, which is shorter than its diff:
```python
import functools
import math

import jax
import jax.numpy as jnp
from jax import lax
from jax.experimental import pallas as pl
from jax.experimental.pallas import tpu as pltpu
from jax.sharding import PartitionSpec as P

MESH = pl.DeviceIdType.MESH
BF = jnp.bfloat16
F32 = jnp.float32

NF = 4
R = 4
X = 128
C = 128
H = NF * R
D = X + 16
E = X + 32
MSG = R * X + 128


def dot(a, b):
    return jnp.dot(a, b, preferred_element_type=F32)


def dot_t(a, b):
    return lax.dot_general(a, b, (((1,), (1,)), ((), ())), preferred_element_type=F32)


def kernel(
    ntm,
    ncol,
    kidx,
    feat,
    keys,
    mw,
    jw,
    dw,
    fw,
    out,
    F,
    KK,
    FE,
    ES_K,
    ES_F,
    EK,
    EF,
    SB,
    RB,
    PM,
    FQ,
    KR,
    CB,
    WB,
    J3,
    W1,
    H3,
    W2,
    HB,
    OS,
    RO,
    loc_sem,
    w_sem,
    ksend,
    krecv,
    esend,
    erecv,
    fsend,
    frecv,
    msend,
    mrecv,
    osend,
    orecv,
):
    tm = lax.axis_index("tm")
    row = lax.axis_index("row")
    col = lax.axis_index("col")
    nrow = NF
    tm_next = lax.rem(tm + 1, ntm)
    tm_prev = lax.rem(tm + ntm - 1, ntm)
    has_left = col > 0
    has_right = col < ncol - 1

    own_key = pltpu.make_async_copy(keys.at[0], KK.at[1], loc_sem.at[0])
    own_key.start()
    edge_l = pltpu.make_async_copy(feat.at[:, :, pl.ds(0, 16), :], FE.at[0], loc_sem.at[1])
    edge_l.start()
    edge_r = pltpu.make_async_copy(feat.at[:, :, pl.ds(X - 16, 16), :], FE.at[1], loc_sem.at[2])
    edge_r.start()
    own_feat = pltpu.make_async_copy(feat.at[row], F.at[row], loc_sem.at[3])
    own_feat.start()
    weights = []
    for i in range(3):
        for o in range(2):
            weights.append(
                pltpu.make_async_copy(jw.at[i], W1.at[i + o, :, pl.ds(128 * o, 128)], w_sem.at[0, i, o])
            )
            weights.append(
                pltpu.make_async_copy(dw.at[i], W2.at[i + o, :, pl.ds(128 * o, 128)], w_sem.at[1, i, o])
            )
    for w in weights:
        w.start()

    bar = pltpu.get_barrier_semaphore()

    def greet(t, r, c):
        pl.semaphore_signal(bar, inc=1, device_id=(t, r, c), device_id_type=MESH)

    for o in range(1, nrow):
        greet(tm, lax.rem(row + o, nrow), col)
    greet(tm_prev, row, col)

    @pl.when(has_left)
    def _():
        greet(tm, row, col - 1)
        greet(tm_prev, row, col - 1)

    @pl.when(has_right)
    def _():
        greet(tm, row, col + 1)
        greet(tm_prev, row, col + 1)

    pl.semaphore_wait(bar, nrow + 2 * has_left.astype(jnp.int32) + 2 * has_right.astype(jnp.int32))

    def remote(src, dst, s, r, dev):
        return pltpu.make_async_remote_copy(
            src_ref=src, dst_ref=dst, send_sem=s, recv_sem=r, device_id=dev, device_id_type=MESH
        )

    key_copy = remote(keys.at[0], KK.at[0], ksend, krecv, (tm_next, row, col))
    key_copy.start()
    feat_copies = []
    for o in (2, 1, 3):
        there = lax.rem(row + o, nrow)
        cp = remote(feat.at[there], F.at[row], fsend.at[o - 1], frecv.at[o - 1], (tm, there, col))
        cp.start()
        feat_copies.append(cp)

    own_key.wait()
    edge_l.wait()
    edge_r.wait()
    for side in range(2):
        kv = KK[1, :, X - 16 :, :] if side else KK[1, :, :16, :]
        kv = kv.astype(F32)[:, 8 * side : 8 * side + 8, :]
        ES_K[side] = kv.reshape(R * 8, C).astype(BF)
        for f in range(NF):
            fv = FE[side, f].astype(F32)[:, 8 * side : 8 * side + 8, :]
            ES_F[side, f] = fv.reshape(R * 8, C).astype(BF)

    def edge_copies(side):
        other = 1 - side
        c = col + 2 * side - 1
        return [
            remote(ES_K.at[side], EK.at[0, other], esend.at[side, 0], erecv.at[other, 0], (tm_next, row, c)),
            remote(ES_K.at[side], EK.at[1, other], esend.at[side, 1], erecv.at[other, 1], (tm, row, c)),
            remote(ES_F.at[side], EF.at[other], esend.at[side, 2], erecv.at[other, 2], (tm, row, c)),
        ]

    def edge_waits(side):
        c = col + 2 * side - 1
        return [
            remote(ES_K.at[side], EK.at[0, side], esend.at[side, 0], erecv.at[side, 0], (tm_next, row, c)),
            remote(ES_K.at[side], EK.at[1, side], esend.at[side, 1], erecv.at[side, 1], (tm, row, c)),
            remote(ES_F.at[side], EF.at[side], esend.at[side, 2], erecv.at[side, 2], (tm, row, c)),
        ]

    for side, has in ((0, has_left), (1, has_right)):

        @pl.when(has)
        def _(side=side):
            for cp in edge_copies(side):
                cp.start()

    q = lax.broadcasted_iota(jnp.int32, (144, 81), 0)
    d = lax.broadcasted_iota(jnp.int32, (144, 81), 1)
    t = q & 15
    pick = (d == 9 * (q >> 4) + 15 - t) & (t >= 7)
    WB[...] = jnp.zeros_like(WB)
    WB[176:320, :] = dot(pick.astype(F32).astype(BF), mw[...]).astype(BF)

    e = lax.broadcasted_iota(jnp.int32, (E, 192), 0)
    s = lax.broadcasted_iota(jnp.int32, (E, 192), 1)
    for yy in range(R):
        in_row = ((s >> 3) & 3) == yy
        x = jnp.where(s < X, s, jnp.where(s < X + 32, (s & 7) - 8, (s & 7) + X))
        keep = (x == 139 - e) & ((s < X) | in_row)
        PM[yy] = keep.astype(F32).astype(BF)

    zero = jnp.zeros((768, 128), BF)
    W1[0, :, 128:256] = zero
    W1[3, :, 0:128] = zero
    W2[0, :, 128:256] = zero[:384]
    W2[3, :, 0:128] = zero[:384]
    for i in (0, H + 1):
        J3[i] = jnp.zeros((D, 768), BF)
        HB[i] = jnp.zeros((X, 384), BF)
    for i in (0, 1, H + 2, H + 3):
        H3[i] = jnp.zeros((D, 384), BF)

    dd = lax.broadcasted_iota(jnp.int32, (D, C), 0)
    inside = (has_left | (dd >= 8)) & (has_right | (dd < X + 8))

    krecv_wait = remote(keys.at[0], KK.at[0], ksend, krecv, (tm_next, row, col))
    krecv_wait.wait()
    for side, has in ((0, has_left), (1, has_right)):

        @pl.when(has)
        def _(side=side):
            for cp in edge_waits(side):
                cp.wait_recv()

    def fill(dst, frame):
        slot = jnp.where(kidx[frame, 0] == tm, 1, 0)
        for yy in range(R):
            dst[X * yy : X * yy + X, :] = KK[slot, yy]
        for side in range(2):
            dst[R * X + 32 * side : R * X + 32 * side + 32, :] = EK[slot, side]
            dst[R * X + 64 + 32 * side : R * X + 96 + 32 * side, :] = EF[side, frame]

    msg_copies = []
    for o in (2, 1, 3):
        there = lax.rem(row + o, nrow)
        fill(SB.at[o - 1], there)
        cp = remote(SB.at[o - 1], RB.at[row], msend.at[o - 1], mrecv.at[o - 1], (tm, there, col))
        cp.start()
        msg_copies.append(cp)
    fill(RB.at[row], row)

    own_feat.wait()
    for cp in feat_copies:
        cp.wait_recv()
    for w in weights:
        w.wait()
    for cp in msg_copies:
        cp.wait_recv()

    hrow = lax.broadcasted_iota(jnp.int32, (64, C), 0)
    border = jnp.where(hrow < 32, has_left.astype(jnp.int32), has_right.astype(jnp.int32)) == 1

    def arrange(rs, carry):
        kh = jnp.where(border, RB[rs, R * X : R * X + 64, :].astype(F32), 0.0).astype(BF)
        fh = jnp.where(border, RB[rs, R * X + 64 : R * X + 128, :].astype(F32), 0.0)
        for yy in range(R):
            y = R * rs + yy
            src = jnp.concatenate([RB[rs, X * yy : X * yy + X, :], kh], axis=0)
            KR[y] = dot(PM[yy], src)
            fr = jnp.concatenate(
                [fh[8 * yy : 8 * yy + 8], F[rs, yy].astype(F32), fh[32 + 8 * yy : 40 + 8 * yy]], axis=0
            )
            FQ[y] = fr
            for j in range(3):
                sh = fr if j == 1 else pltpu.roll(fr, (1 - j) % D, 0)
                J3[y + 1, :, 256 * j + 128 : 256 * j + 256] = sh.astype(BF)
        return carry

    lax.fori_loop(0, NF, arrange, 0)

    scale = 1.0 / math.sqrt(C)

    def correlate(p, carry):
        parts = []
        for h in range(2):
            d0 = pl.multiple_of(16 * p + 8 * h, 8)
            e0 = pl.multiple_of(136 - 16 * p - 8 * h, 8)
            qs = FQ[:, pl.ds(d0, 8), :].reshape(H * 8, C).astype(BF)
            ks = KR[:, pl.ds(e0, 16), :].reshape(H * 16, C).astype(BF)
            sc = dot_t(qs, ks).reshape(H, 8, 256) * scale
            lo = pltpu.roll(sc[:, :, :128], 0, 2, stride=1, stride_axis=1)
            hi = pltpu.roll(sc[:, :, 128:], 0, 2, stride=1, stride_axis=1)
            parts.append(jnp.concatenate([lo, hi], axis=2))
        c0 = pl.multiple_of(16 * p, 16)
        CB[:, pl.ds(c0, 16), :] = jnp.concatenate(parts, axis=1).astype(BF)
        return carry

    lax.fori_loop(0, D // 16, correlate, 0)

    def motion(y, carry):
        w0 = pl.multiple_of(16 * (15 - y), 16)
        m = dot(CB[y], WB[pl.ds(w0, 256), :])
        m = jnp.where(inside, jnp.maximum(m, 0.0), 0.0)
        for j in range(3):
            sh = m if j == 1 else pltpu.roll(m, (1 - j) % D, 0)
            J3[y + 1, :, 256 * j : 256 * j + 128] = sh.astype(BF)
        return carry

    lax.fori_loop(0, H, motion, 0)

    def joint(p, carry):
        lhs = jnp.concatenate([J3[2 * p + t] for t in range(4)], axis=1)
        h = dot(lhs, W1[...].reshape(4 * 768, 256))
        for o in range(2):
            ho = jnp.where(inside, jnp.maximum(h[:, 128 * o : 128 * o + 128], 0.0), 0.0)
            for j in range(3):
                sh = ho if j == 1 else pltpu.roll(ho, (2 - 2 * j) % D, 0)
                H3[2 * p + o + 2, :, 128 * j : 128 * j + 128] = sh.astype(BF)
        return carry

    lax.fori_loop(0, H // 2, joint, 0)

    def dilated(p, carry):
        y0 = 4 * (p // 2) + lax.rem(p, 2)
        lhs = jnp.concatenate([H3[y0 + 2 * t] for t in range(4)], axis=1)
        h = dot(lhs, W2[...].reshape(4 * 384, 256))
        for o in range(2):
            ho = jnp.where(inside, jnp.maximum(h[:, 128 * o : 128 * o + 128], 0.0), 0.0)
            for j in range(3):
                sh = pltpu.roll(ho, (-7 - j) % D, 0)[:X]
                HB[y0 + 2 * o + 1, :, 128 * j : 128 * j + 128] = sh.astype(BF)
        return carry

    lax.fori_loop(0, H // 2, dilated, 0)

    def head(rr, carry):
        for yy in range(R):
            y = R * rr + yy
            rhs = jnp.concatenate([HB[y + i] for i in range(3)], axis=1)
            res = dot_t(fw[...], rhs)
            OS[rr, :, yy : yy + 1, :] = res.reshape(2, 1, X)
        return carry

    lax.fori_loop(0, NF, head, 0)

    out_copies = []
    for o in range(1, nrow):
        there = lax.rem(row + o, nrow)
        cp = remote(OS.at[there], RO.at[row], osend.at[o - 1], orecv.at[o - 1], (tm, there, col))
        cp.start()
        out_copies.append(cp)
    RO[row] = OS[row]
    for cp in out_copies:
        cp.wait_recv()
    out[...] = RO[...]

    for cp in feat_copies + msg_copies + out_copies:
        cp.wait_send()
    for side, has in ((0, has_left), (1, has_right)):

        @pl.when(has)
        def _(side=side):
            for cp in edge_copies(side):
                cp.wait_send()


def solution(mesh):
    ntm, ncol = mesh.shape["tm"], mesh.shape["col"]

    def step(feat, keys, kidx, mw, jw, dw, fw):
        anyspec = pl.BlockSpec(memory_space=pltpu.HBM)
        vspec = pl.BlockSpec(memory_space=pltpu.VMEM)
        dma = pltpu.SemaphoreType.DMA
        return pl.pallas_call(
            functools.partial(kernel, ntm, ncol),
            out_shape=jax.ShapeDtypeStruct((NF, 2, R, X), F32),
            in_specs=[
                pl.BlockSpec(memory_space=pltpu.SMEM),
                anyspec,
                anyspec,
                vspec,
                anyspec,
                anyspec,
                vspec,
            ],
            out_specs=vspec,
            scratch_shapes=[
                pltpu.VMEM((NF, R, X, C), BF),
                pltpu.VMEM((2, R, X, C), BF),
                pltpu.VMEM((2, NF, R, 16, C), BF),
                pltpu.VMEM((2, R * 8, C), BF),
                pltpu.VMEM((2, NF, R * 8, C), BF),
                pltpu.VMEM((2, 2, R * 8, C), BF),
                pltpu.VMEM((2, NF, R * 8, C), BF),
                pltpu.VMEM((3, MSG, C), BF),
                pltpu.VMEM((NF, MSG, C), BF),
                pltpu.VMEM((R, E, 192), BF),
                pltpu.VMEM((H, D, C), F32),
                pltpu.VMEM((H, E, C), F32),
                pltpu.VMEM((H, D, 256), BF),
                pltpu.VMEM((31 * 16, C), BF),
                pltpu.VMEM((H + 2, D, 768), BF),
                pltpu.VMEM((4, 768, 256), BF),
                pltpu.VMEM((H + 4, D, 384), BF),
                pltpu.VMEM((4, 384, 256), BF),
                pltpu.VMEM((H + 2, X, 384), BF),
                pltpu.VMEM((NF, 2, R, X), F32),
                pltpu.VMEM((NF, 2, R, X), F32),
                dma((4,)),
                dma((2, 3, 2)),
                dma,
                dma,
                dma((2, 3)),
                dma((2, 3)),
                dma((3,)),
                dma((3,)),
                dma((3,)),
                dma((3,)),
                dma((3,)),
                dma((3,)),
            ],
            compiler_params=pltpu.CompilerParams(
                collective_id=0, has_side_effects=True, vmem_limit_bytes=48 * 1024 * 1024
            ),
        )(
            kidx,
            feat,
            keys,
            mw,
            jw.reshape(3, 768, 128),
            dw.reshape(3, 384, 128),
            fw.reshape(2, 1152),
        )

    in_specs = (
        P("tm", "row", "col", None),
        P("tm", "row", "col", None),
        P("tm", None),
        P(),
        P(),
        P(),
        P(),
    )
    return jax.shard_map(
        step, mesh=mesh, in_specs=in_specs, out_specs=P("tm", None, "row", "col"), check_vma=False
    )
```

time: 201 us -> 49.6 us (0.25)
  starting transfers between devices: 57.2 us -> 0 us
  matrix products: 45.8 us -> 0 us
  Pallas kernels: 0 us -> 43.2 us
  local copies, waits for them, and re-layouts: 43.6 us -> 6.07 us
  waiting for transfers between devices: 30.8 us -> 0 us
  other arithmetic: 20.7 us -> 0 us
    ppermute x17 -> x0, starting transfers between devices: 57.2 us -> none  [the longest x8 41.7 us: extended(): lax.ppermute(tail, axis, [(i, (i + 1) % count) for i in range(ends)])]
    dot_general x45 -> x0, matrix products: 45.8 us -> none  [the longest x9 22.2 us: correlate(): jnp.einsum('fyxc,fvxc->fyvx', queries, window, preferred_element_type=jnp...]
    pallas_call x0 -> x1, Pallas kernels: none -> 43.2 us  [step(): pl.pallas_call(functools.partial(kernel, ntm, ncol), out_shape=jax.ShapeD...]
    ppermute x17 -> x0, waiting for transfers between devices: 30.8 us -> none  [the longest x8 28.8 us: extended(): lax.ppermute(head, axis, [((i + 1) % count, i) for i in range(ends)])]
    slice x30 -> x0, local copies, waits for them, and re-layouts: 24.7 us -> none  [the longest x9 12 us: correlate(): weight_rows = motion_weight[shift_column::window_size]]
    dot_general x9 -> x0, other arithmetic: 14.1 us -> none  [correlate(): jnp.einsum('fyxc,fvxc->fyvx', queries, window, preferred_element_type=jnp...]
    concatenate x7 -> x0, other arithmetic: 6.5 us -> none  [the longest x6 6.37 us: extended(): jnp.concatenate([lax.ppermute(tail, axis, [(i, (i + 1) % count) for i in...]
    ppermute x6 -> x0, local copies, waits for them, and re-layouts: 4.43 us -> none  [the longest x3 2.51 us: extended(): lax.ppermute(head, axis, [((i + 1) % count, i) for i in range(ends)])]
  transfers between devices with their start and end apart: 17 -> 0, of which waited for: 10 -> 0; matrix products, arithmetic and copies ran while one was open for 16% -> 0% of each run, Pallas kernels for 0% -> 0%
where the time goes in v1:
time: 49.6 us; the launch traced here: 49.3 us
  Pallas kernels  43.2 us (87%)
  local copies, waits for them, and re-layouts  6.07 us (12%)
    pallas_call x1, Pallas kernels, step(): pl.pallas_call(functools.partial(kernel, ntm, ncol), out_shape=jax.ShapeD...  43.2 us
    unnamed x16, local copies, waits for them, and re-layouts  6.07 us

profile of v1, /device:TPU:1, one launch (start us, length us, event | category | flops | bytes accessed | tf_op | source)
XLA Modules:
  0.0 49.3 jit_solution(11416702356210565890)
XLA Ops:
  0.0 0.0 copy-start.5
  0.0 0.0 copy-start.6
  0.0 0.7 %copy-done.6 = s32[4,1]{0,1:T(1,128)S(1)} copy-done((s32[4,1]{0,1:T(1,128)S(1)}, s32[4,1]{0,1:T(1,128)}, u32[]{:S(2)}) %copy-start.6) | copy-done | bytes 40
  0.7 0.1 copy.11.kidx
  0.8 0.0 copy-done.5
  0.8 0.0 copy-start
  0.8 1.1 %copy-done = bf16[3,3,256,128]{3,2,1,0:T(8,128)(2,1)S(1)} copy-done((bf16[3,3,256,128]{3,2,1,0:T(8,128)(2,1)S(1)}, bf16[3,3,256,128]{3,2,1,0:T(8,128)(2,1)}, u32[]{:S(2)}) %copy-start) | copy-done | bytes 589848
  1.8 0.0 copy-start.1
  1.8 1.0 %copy-done.1 = bf16[4,4,128,128]{3,2,1,0:T(8,128)(2,1)S(1)} copy-done((bf16[4,4,128,128]{3,2,1,0:T(8,128)(2,1)S(1)}, bf16[4,4,128,128]{3,2,1,0:T(8,128)(2,1)}, u32[]{:S(2)}) %copy-start.1) | copy-done | bytes 524312
  2.9 0.0 copy-start.2
  2.9 1.0 %copy-done.2 = bf16[3,3,128,128]{3,2,1,0:T(8,128)(2,1)S(1)} copy-done((bf16[3,3,128,128]{3,2,1,0:T(8,128)(2,1)S(1)}, bf16[3,3,128,128]{3,2,1,0:T(8,128)(2,1)}, u32[]{:S(2)}) %copy-start.2) | copy-done | bytes 294936
  3.8 0.0 copy-start.3
  3.8 0.9 %copy-done.3 = bf16[1,4,128,128]{3,2,1,0:T(8,128)(2,1)S(1)} copy-done((bf16[1,4,128,128]{3,2,1,0:T(8,128)(2,1)S(1)}, bf16[1,4,128,128]{3,2,1,0:T(8,128)(2,1)}, u32[]{:S(2)}) %copy-start.3) | copy-done | bytes 131096
  4.7 0.0 copy-start.4
  4.7 0.7 %copy-done.4 = bf16[81,128]{1,0:T(8,128)(2,1)S(1)} copy-done((bf16[81,128]{1,0:T(8,128)(2,1)S(1)}, bf16[81,128]{1,0:T(8,128)(2,1)}, u32[]{:S(2)}) %copy-start.4) | copy-done | bytes 20760
  5.5 43.2 %shard_map.73 = f32[4,2,4,128]{3,2,1,0:T(4,128)S(1)} custom-call(s32[4,1]{1,0:T(4,128)S(1)} %copy.11.kidx, bf16[4,4,128,128]{3,2,1,0:T(8,128)(2,1)S(1)} %copy-done.1, bf16[1,4,128,128]{3,2,1,0:T(8,128)(2,1)S(1)} %copy-done.3, bf16[81,128]{1,0:T(8,128)(2,1)S(1)} %copy-done.4, bf16[3,768,128]{2,1,0:T(8,128)(2,1)S(1)} %bitcast.3, ...), custom_call_target="tpu_custom_call" | custom-call | tf_op jit(solution)/shard_map/pallas_call | solution.py:354
  48.7 0.6 %copy.13 = f32[4,2,4,128]{3,2,1,0:T(4,128)} copy(f32[4,2,4,128]{3,2,1,0:T(4,128)S(1)} %shard_map.73) | data formatting | bytes 32768
Async XLA Ops:
  0.0 0.8 %copy-start.5 = (bf16[2,3,3,128]{3,0,2,1:T(2,128)(2,1)S(1)}, bf16[2,3,3,128]{3,0,2,1:T(2,128)(2,1)}, u32[]{:S(2)}) copy-start(bf16[2,3,3,128]{3,0,2,1:T(2,128)(2,1)} %param.13) | copy-start | bytes 13828
  0.0 0.7 %copy-start.6 = (s32[4,1]{0,1:T(1,128)S(1)}, s32[4,1]{0,1:T(1,128)}, u32[]{:S(2)}) copy-start(s32[4,1]{0,1:T(1,128)} %param.9) | copy-start | bytes 52
  0.8 1.1 %copy-start = (bf16[3,3,256,128]{3,2,1,0:T(8,128)(2,1)S(1)}, bf16[3,3,256,128]{3,2,1,0:T(8,128)(2,1)}, u32[]{:S(2)}) copy-start(bf16[3,3,256,128]{3,2,1,0:T(8,128)(2,1)} %param.11) | copy-start | bytes 1769476
  1.8 1.0 %copy-start.1 = (bf16[4,4,128,128]{3,2,1,0:T(8,128)(2,1)S(1)}, bf16[4,4,128,128]{3,2,1,0:T(8,128)(2,1)}, u32[]{:S(2)}) copy-start(bf16[4,4,128,128]{3,2,1,0:T(8,128)(2,1)} %feat.1) | copy-start | bytes 1572868
  2.9 1.0 %copy-start.2 = (bf16[3,3,128,128]{3,2,1,0:T(8,128)(2,1)S(1)}, bf16[3,3,128,128]{3,2,1,0:T(8,128)(2,1)}, u32[]{:S(2)}) copy-start(bf16[3,3,128,128]{3,2,1,0:T(8,128)(2,1)} %param.12) | copy-start | bytes 884740
  3.8 0.9 %copy-start.3 = (bf16[1,4,128,128]{3,2,1,0:T(8,128)(2,1)S(1)}, bf16[1,4,128,128]{3,2,1,0:T(8,128)(2,1)}, u32[]{:S(2)}) copy-start(bf16[1,4,128,128]{3,2,1,0:T(8,128)(2,1)} %keys.1) | copy-start | bytes 393220
  4.7 0.7 %copy-start.4 = (bf16[81,128]{1,0:T(8,128)(2,1)S(1)}, bf16[81,128]{1,0:T(8,128)(2,1)}, u32[]{:S(2)}) copy-start(bf16[81,128]{1,0:T(8,128)(2,1)} %mw.1) | copy-start | bytes 62212

commit v2 on v1

--- a/solution.py
+++ b/solution.py
@@ -19,7 +19,7 @@
 H = NF * R
 D = X + 16
 E = X + 32
-MSG = R * X + 128
+MSG = R * X
 
 
 def dot(a, b):
@@ -50,6 +50,10 @@
     EF,
     SB,
     RB,
+    SH,
+    RH,
+    MW,
+    FW,
     PM,
     FQ,
     KR,
@@ -72,6 +76,9 @@
     frecv,
     msend,
     mrecv,
+    hsend,
+    hrecv,
+    ready,
     osend,
     orecv,
 ):
@@ -84,25 +91,15 @@
     has_left = col > 0
     has_right = col < ncol - 1
 
-    own_key = pltpu.make_async_copy(keys.at[0], KK.at[1], loc_sem.at[0])
-    own_key.start()
-    edge_l = pltpu.make_async_copy(feat.at[:, :, pl.ds(0, 16), :], FE.at[0], loc_sem.at[1])
-    edge_l.start()
-    edge_r = pltpu.make_async_copy(feat.at[:, :, pl.ds(X - 16, 16), :], FE.at[1], loc_sem.at[2])
-    edge_r.start()
-    own_feat = pltpu.make_async_copy(feat.at[row], F.at[row], loc_sem.at[3])
-    own_feat.start()
-    weights = []
-    for i in range(3):
-        for o in range(2):
-            weights.append(
-                pltpu.make_async_copy(jw.at[i], W1.at[i + o, :, pl.ds(128 * o, 128)], w_sem.at[0, i, o])
-            )
-            weights.append(
-                pltpu.make_async_copy(dw.at[i], W2.at[i + o, :, pl.ds(128 * o, 128)], w_sem.at[1, i, o])
-            )
-    for w in weights:
-        w.start()
+    def local(src, dst, sem):
+        cp = pltpu.make_async_copy(src, dst, sem)
+        cp.start()
+        return cp
+
+    cross_left = has_left & (lax.rem(col, 2) == 0)
+    cross_right = has_right & (lax.rem(col, 2) == 1)
+    near_left = has_left & (lax.rem(col, 2) == 1)
+    near_right = has_right & (lax.rem(col, 2) == 0)
 
     bar = pltpu.get_barrier_semaphore()
 
@@ -113,31 +110,31 @@
         greet(tm, lax.rem(row + o, nrow), col)
     greet(tm_prev, row, col)
 
-    @pl.when(has_left)
+    @pl.when(cross_right)
+    def _():
+        greet(tm, row, col + 1)
+        greet(tm_prev, row, col + 1)
+        greet(tm_next, row, col + 1)
+
+    @pl.when(near_left)
     def _():
         greet(tm, row, col - 1)
         greet(tm_prev, row, col - 1)
 
-    @pl.when(has_right)
+    @pl.when(near_right)
     def _():
         greet(tm, row, col + 1)
         greet(tm_prev, row, col + 1)
 
-    pl.semaphore_wait(bar, nrow + 2 * has_left.astype(jnp.int32) + 2 * has_right.astype(jnp.int32))
-
-    def remote(src, dst, s, r, dev):
-        return pltpu.make_async_remote_copy(
-            src_ref=src, dst_ref=dst, send_sem=s, recv_sem=r, device_id=dev, device_id_type=MESH
-        )
-
-    key_copy = remote(keys.at[0], KK.at[0], ksend, krecv, (tm_next, row, col))
-    key_copy.start()
-    feat_copies = []
-    for o in (2, 1, 3):
-        there = lax.rem(row + o, nrow)
-        cp = remote(feat.at[there], F.at[row], fsend.at[o - 1], frecv.at[o - 1], (tm, there, col))
-        cp.start()
-        feat_copies.append(cp)
+    own_key = local(keys.at[0], KK.at[1], loc_sem.at[0])
+    edge_l = local(feat.at[:, :, pl.ds(0, 16), :], FE.at[0], loc_sem.at[1])
+    edge_r = local(feat.at[:, :, pl.ds(X - 16, 16), :], FE.at[1], loc_sem.at[2])
+    own_feat = local(feat.at[row], F.at[row], loc_sem.at[3])
+    weights = [local(mw, MW, loc_sem.at[4]), local(fw, FW, loc_sem.at[5])]
+    for i in range(3):
+        for o in range(2):
+            weights.append(local(jw.at[i], W1.at[i + o, :, pl.ds(128 * o, 128)], w_sem.at[0, i, o]))
+            weights.append(local(dw.at[i], W2.at[i + o, :, pl.ds(128 * o, 128)], w_sem.at[1, i, o]))
 
     own_key.wait()
     edge_l.wait()
@@ -150,6 +147,19 @@
             fv = FE[side, f].astype(F32)[:, 8 * side : 8 * side + 8, :]
             ES_F[side, f] = fv.reshape(R * 8, C).astype(BF)
 
+    one = lambda flag, n: n * flag.astype(jnp.int32)
+    pl.semaphore_wait(bar, nrow + one(near_left, 2) + one(near_right, 2) + one(cross_left, 3))
+
+    @pl.when(cross_left)
+    def _():
+        for t in (tm, tm_prev):
+            pl.semaphore_signal(ready, inc=1, device_id=(t, row, col - 1), device_id_type=MESH)
+
+    def remote(src, dst, s, r, dev):
+        return pltpu.make_async_remote_copy(
+            src_ref=src, dst_ref=dst, send_sem=s, recv_sem=r, device_id=dev, device_id_type=MESH
+        )
+
     def edge_copies(side):
         other = 1 - side
         c = col + 2 * side - 1
@@ -167,19 +177,30 @@
             remote(ES_F.at[side], EF.at[side], esend.at[side, 2], erecv.at[side, 2], (tm, row, c)),
         ]
 
-    for side, has in ((0, has_left), (1, has_right)):
-
-        @pl.when(has)
+    for side, go in ((0, has_left), (1, near_right)):
+
+        @pl.when(go)
         def _(side=side):
             for cp in edge_copies(side):
                 cp.start()
 
+    key_copy = remote(keys.at[0], KK.at[0], ksend, krecv, (tm_next, row, col))
+    key_copy.start()
+    feat_copies = []
+    for o in (2, 1, 3):
+        there = lax.rem(row + o, nrow)
+        cp = remote(feat.at[there], F.at[row], fsend.at[o - 1], frecv.at[o - 1], (tm, there, col))
+        cp.start()
+        feat_copies.append(cp)
+
+    for w in weights:
+        w.wait()
     q = lax.broadcasted_iota(jnp.int32, (144, 81), 0)
     d = lax.broadcasted_iota(jnp.int32, (144, 81), 1)
     t = q & 15
     pick = (d == 9 * (q >> 4) + 15 - t) & (t >= 7)
     WB[...] = jnp.zeros_like(WB)
-    WB[176:320, :] = dot(pick.astype(F32).astype(BF), mw[...]).astype(BF)
+    WB[176:320, :] = dot(pick.astype(F32).astype(BF), MW[...]).astype(BF)
 
     e = lax.broadcasted_iota(jnp.int32, (E, 192), 0)
     s = lax.broadcasted_iota(jnp.int32, (E, 192), 1)
@@ -203,22 +224,21 @@
     dd = lax.broadcasted_iota(jnp.int32, (D, C), 0)
     inside = (has_left | (dd >= 8)) & (has_right | (dd < X + 8))
 
-    krecv_wait = remote(keys.at[0], KK.at[0], ksend, krecv, (tm_next, row, col))
-    krecv_wait.wait()
-    for side, has in ((0, has_left), (1, has_right)):
-
-        @pl.when(has)
-        def _(side=side):
-            for cp in edge_waits(side):
-                cp.wait_recv()
+    key_copy.wait()
+
+    def slot_of(frame):
+        return jnp.where(kidx[frame] == tm, 1, 0)
 
     def fill(dst, frame):
-        slot = jnp.where(kidx[frame, 0] == tm, 1, 0)
+        slot = slot_of(frame)
         for yy in range(R):
             dst[X * yy : X * yy + X, :] = KK[slot, yy]
+
+    def fill_border(dst, frame):
+        slot = slot_of(frame)
         for side in range(2):
-            dst[R * X + 32 * side : R * X + 32 * side + 32, :] = EK[slot, side]
-            dst[R * X + 64 + 32 * side : R * X + 96 + 32 * side, :] = EF[side, frame]
+            dst[32 * side : 32 * side + 32, :] = EK[slot, side]
+            dst[64 + 32 * side : 96 + 32 * side, :] = EF[side, frame]
 
     msg_copies = []
     for o in (2, 1, 3):
@@ -229,20 +249,38 @@
         msg_copies.append(cp)
     fill(RB.at[row], row)
 
+    @pl.when(cross_right)
+    def _():
+        pl.semaphore_wait(ready, 2)
+        for cp in edge_copies(1):
+            cp.start()
+
+    for side, has in ((0, has_left), (1, has_right)):
+
+        @pl.when(has)
+        def _(side=side):
+            for cp in edge_waits(side):
+                cp.wait_recv()
+
+    border_copies = []
+    for o in (2, 1, 3):
+        there = lax.rem(row + o, nrow)
+        fill_border(SH.at[o - 1], there)
+        cp = remote(SH.at[o - 1], RH.at[row], hsend.at[o - 1], hrecv.at[o - 1], (tm, there, col))
+        cp.start()
+        border_copies.append(cp)
+    fill_border(RH.at[row], row)
+
     own_feat.wait()
-    for cp in feat_copies:
-        cp.wait_recv()
-    for w in weights:
-        w.wait()
-    for cp in msg_copies:
+    for cp in feat_copies + msg_copies + border_copies:
         cp.wait_recv()
 
     hrow = lax.broadcasted_iota(jnp.int32, (64, C), 0)
     border = jnp.where(hrow < 32, has_left.astype(jnp.int32), has_right.astype(jnp.int32)) == 1
 
     def arrange(rs, carry):
-        kh = jnp.where(border, RB[rs, R * X : R * X + 64, :].astype(F32), 0.0).astype(BF)
-        fh = jnp.where(border, RB[rs, R * X + 64 : R * X + 128, :].astype(F32), 0.0)
+        kh = jnp.where(border, RH[rs, :64, :].astype(F32), 0.0).astype(BF)
+        fh = jnp.where(border, RH[rs, 64:, :].astype(F32), 0.0)
         for yy in range(R):
             y = R * rs + yy
             src = jnp.concatenate([RB[rs, X * yy : X * yy + X, :], kh], axis=0)
@@ -317,7 +355,7 @@
         for yy in range(R):
             y = R * rr + yy
             rhs = jnp.concatenate([HB[y + i] for i in range(3)], axis=1)
-            res = dot_t(fw[...], rhs)
+            res = dot_t(FW[...], rhs)
             OS[rr, :, yy : yy + 1, :] = res.reshape(2, 1, X)
         return carry
 
@@ -334,7 +372,7 @@
         cp.wait_recv()
     out[...] = RO[...]
 
-    for cp in feat_copies + msg_copies + out_copies:
+    for cp in feat_copies + msg_copies + border_copies + out_copies:
         cp.wait_send()
     for side, has in ((0, has_left), (1, has_right)):
 
@@ -358,10 +396,10 @@
                 pl.BlockSpec(memory_space=pltpu.SMEM),
                 anyspec,
                 anyspec,
-                vspec,
-                anyspec,
-                anyspec,
-                vspec,
+                anyspec,
+                anyspec,
+                anyspec,
+                anyspec,
             ],
             out_specs=vspec,
             scratch_shapes=[
@@ -374,6 +412,10 @@
                 pltpu.VMEM((2, NF, R * 8, C), BF),
                 pltpu.VMEM((3, MSG, C), BF),
                 pltpu.VMEM((NF, MSG, C), BF),
+                pltpu.VMEM((3, 128, C), BF),
+                pltpu.VMEM((NF, 128, C), BF),
+                pltpu.VMEM((81, C), BF),
+                pltpu.VMEM((2, 9 * C), BF),
                 pltpu.VMEM((R, E, 192), BF),
                 pltpu.VMEM((H, D, C), F32),
                 pltpu.VMEM((H, E, C), F32),
@@ -386,7 +428,7 @@
                 pltpu.VMEM((H + 2, X, 384), BF),
                 pltpu.VMEM((NF, 2, R, X), F32),
                 pltpu.VMEM((NF, 2, R, X), F32),
-                dma((4,)),
+                dma((6,)),
                 dma((2, 3, 2)),
                 dma,
                 dma,
@@ -398,12 +440,15 @@
                 dma((3,)),
                 dma((3,)),
                 dma((3,)),
+                pltpu.SemaphoreType.REGULAR,
+                dma((3,)),
+                dma((3,)),
             ],
             compiler_params=pltpu.CompilerParams(
-                collective_id=0, has_side_effects=True, vmem_limit_bytes=48 * 1024 * 1024
+                collective_id=0, has_side_effects=True, vmem_limit_bytes=60 * 1024 * 1024
             ),
         )(
-            kidx,
+            kidx.reshape(NF),
             feat,
             keys,
             mw,

time: 49.6 us -> 42 us (0.85)
  local copies, waits for them, and re-layouts: 6.07 us -> 1.32 us
  Pallas kernels: 43.2 us -> 40.5 us
    unnamed x16 -> x1, local copies, waits for them, and re-layouts: 6.07 us -> 1.32 us
    pallas_call x1, Pallas kernels: 43.2 us -> 40.5 us  [step(): pl.pallas_call(functools.partial(kernel, ntm, ncol), out_shape=jax.ShapeD...]
where the time goes in v2:
time: 42 us; the launch traced here: 41.8 us
  Pallas kernels  40.5 us (96%)
  local copies, waits for them, and re-layouts  1.32 us (3%)
    pallas_call x1, Pallas kernels, step(): pl.pallas_call(functools.partial(kernel, ntm, ncol), out_shape=jax.ShapeD...  40.5 us
    unnamed x1, local copies, waits for them, and re-layouts  1.32 us

profile of v2, /device:TPU:1, one launch (start us, length us, event | category | flops | bytes accessed | tf_op | source)
XLA Modules:
  0.0 41.8 jit_solution(13855715191161480015)
XLA Ops:
  0.0 40.5 %shard_map.73 = f32[4,2,4,128]{3,2,1,0:T(4,128)} custom-call(s32[4]{0:T(128)} %bitcast.7, bf16[4,4,128,128]{3,2,1,0:T(8,128)(2,1)} %feat.1, bf16[1,4,128,128]{3,2,1,0:T(8,128)(2,1)} %keys.1, bf16[81,128]{1,0:T(8,128)(2,1)} %mw.1, bf16[3,768,128]{2,1,0:T(8,128)(2,1)} %bitcast.4, bf16[3,384,128]{2,1,0:T(8,128)(2,1)} %bitcast.5, bf16[2,1152]{1,0:T(2,128)(2,1)} %bitcast.6), custom_call_target="tpu_custom_call" | custom-call | tf_op jit(solution)/shard_map/pallas_call | solution.py:392
  40.5 1.3 %copy.11 = f32[4,2,4,128]{3,2,1,0:T(4,128)} copy(f32[4,2,4,128]{3,2,1,0:T(4,128)} %shard_map.73) | data formatting | bytes 32768

commit v3 on v2

--- a/solution.py
+++ b/solution.py
@@ -19,7 +19,8 @@
 H = NF * R
 D = X + 16
 E = X + 32
-MSG = R * X
+NCH = 4
+CH = X // NCH
 
 
 def dot(a, b):
@@ -43,6 +44,7 @@
     out,
     F,
     KK,
+    KV,
     FE,
     ES_K,
     ES_F,
@@ -54,16 +56,20 @@
     RH,
     MW,
     FW,
-    PM,
     FQ,
     KR,
     CB,
-    WB,
-    J3,
-    W1,
+    WR,
+    MF,
+    JF,
+    JM,
+    WF,
+    WM,
+    HF,
     H3,
     W2,
-    HB,
+    W4,
+    RS,
     OS,
     RO,
     loc_sem,
@@ -76,11 +82,11 @@
     frecv,
     msend,
     mrecv,
+    osend,
+    orecv,
+    ready,
     hsend,
     hrecv,
-    ready,
-    osend,
-    orecv,
 ):
     tm = lax.axis_index("tm")
     row = lax.axis_index("row")
@@ -126,22 +132,29 @@
         greet(tm, row, col + 1)
         greet(tm_prev, row, col + 1)
 
-    own_key = local(keys.at[0], KK.at[1], loc_sem.at[0])
+    own_key = local(keys.at[0], KV, loc_sem.at[0])
     edge_l = local(feat.at[:, :, pl.ds(0, 16), :], FE.at[0], loc_sem.at[1])
     edge_r = local(feat.at[:, :, pl.ds(X - 16, 16), :], FE.at[1], loc_sem.at[2])
     own_feat = local(feat.at[row], F.at[row], loc_sem.at[3])
     weights = [local(mw, MW, loc_sem.at[4]), local(fw, FW, loc_sem.at[5])]
     for i in range(3):
         for o in range(2):
-            weights.append(local(jw.at[i], W1.at[i + o, :, pl.ds(128 * o, 128)], w_sem.at[0, i, o]))
-            weights.append(local(dw.at[i], W2.at[i + o, :, pl.ds(128 * o, 128)], w_sem.at[1, i, o]))
+            half = pl.ds(128 * o, 128)
+            weights.append(local(jw.at[i, :, pl.ds(0, C), :], WM.at[i + o, :, :, half], w_sem.at[0, i, o]))
+            weights.append(local(jw.at[i, :, pl.ds(C, C), :], WF.at[i + o, :, :, half], w_sem.at[1, i, o]))
+            weights.append(local(dw.at[i], W2.at[i + o, :, half], w_sem.at[2, i, o]))
 
     own_key.wait()
+    ri = lax.broadcasted_iota(jnp.int32, (X, X), 0)
+    ci = lax.broadcasted_iota(jnp.int32, (X, X), 1)
+    turn = (ri + ci == X - 1).astype(F32).astype(BF)
+    for yy in range(R):
+        KK[1, yy] = dot(turn, KV[yy]).astype(BF)
+
     edge_l.wait()
     edge_r.wait()
     for side in range(2):
-        kv = KK[1, :, X - 16 :, :] if side else KK[1, :, :16, :]
-        kv = kv.astype(F32)[:, 8 * side : 8 * side + 8, :]
+        kv = KK[1, :, :16, :].astype(F32)[:, :8, :] if side else KK[1, :, X - 16 :, :].astype(F32)[:, 8:, :]
         ES_K[side] = kv.reshape(R * 8, C).astype(BF)
         for f in range(NF):
             fv = FE[side, f].astype(F32)[:, 8 * side : 8 * side + 8, :]
@@ -184,7 +197,7 @@
             for cp in edge_copies(side):
                 cp.start()
 
-    key_copy = remote(keys.at[0], KK.at[0], ksend, krecv, (tm_next, row, col))
+    key_copy = remote(KK.at[1], KK.at[0], ksend, krecv, (tm_next, row, col))
     key_copy.start()
     feat_copies = []
     for o in (2, 1, 3):
@@ -195,31 +208,31 @@
 
     for w in weights:
         w.wait()
-    q = lax.broadcasted_iota(jnp.int32, (144, 81), 0)
-    d = lax.broadcasted_iota(jnp.int32, (144, 81), 1)
+    q = lax.broadcasted_iota(jnp.int32, (256, 81), 0)
+    d = lax.broadcasted_iota(jnp.int32, (256, 81), 1)
     t = q & 15
-    pick = (d == 9 * (q >> 4) + 15 - t) & (t >= 7)
-    WB[...] = jnp.zeros_like(WB)
-    WB[176:320, :] = dot(pick.astype(F32).astype(BF), MW[...]).astype(BF)
-
-    e = lax.broadcasted_iota(jnp.int32, (E, 192), 0)
-    s = lax.broadcasted_iota(jnp.int32, (E, 192), 1)
-    for yy in range(R):
-        in_row = ((s >> 3) & 3) == yy
-        x = jnp.where(s < X, s, jnp.where(s < X + 32, (s & 7) - 8, (s & 7) + X))
-        keep = (x == 139 - e) & ((s < X) | in_row)
-        PM[yy] = keep.astype(F32).astype(BF)
-
-    zero = jnp.zeros((768, 128), BF)
-    W1[0, :, 128:256] = zero
-    W1[3, :, 0:128] = zero
-    W2[0, :, 128:256] = zero[:384]
-    W2[3, :, 0:128] = zero[:384]
+    pick = (d == 9 * (q >> 4) + 15 - t) & (t >= 7) & (q < 144)
+    WR[...] = dot(pick.astype(F32).astype(BF), MW[...]).astype(BF)
+
+    zero = jnp.zeros((3, 128, 128), BF)
+    for w in (WM, WF):
+        w[0, :, :, 128:256] = zero
+        w[3, :, :, 0:128] = zero
+    W2[0, :, 128:256] = zero.reshape(384, 128)
+    W2[3, :, 0:128] = zero.reshape(384, 128)
+    for i in range(3):
+        W4[2 * i : 2 * i + 2, :] = FW[:, 384 * i : 384 * i + 384].astype(F32)
+    W4[6:8, :] = jnp.zeros((2, 384), F32)
     for i in (0, H + 1):
-        J3[i] = jnp.zeros((D, 768), BF)
-        HB[i] = jnp.zeros((X, 384), BF)
+        JF[i] = jnp.zeros((D, 384), BF)
+        JM[i] = jnp.zeros((D, 384), BF)
+        RS[i] = jnp.zeros((8, X), F32)
     for i in (0, 1, H + 2, H + 3):
         H3[i] = jnp.zeros((D, 384), BF)
+    KR[:, 0:8, :] = jnp.zeros((H, 8, C), F32)
+    KR[:, E - 16 :, :] = jnp.zeros((H, 16, C), F32)
+    MF[:, 0:8, :] = jnp.zeros((H, 8, C), F32)
+    MF[:, D + 8 :, :] = jnp.zeros((H, 8, C), F32)
 
     dd = lax.broadcasted_iota(jnp.int32, (D, C), 0)
     inside = (has_left | (dd >= 8)) & (has_right | (dd < X + 8))
@@ -228,11 +241,6 @@
 
     def slot_of(frame):
         return jnp.where(kidx[frame] == tm, 1, 0)
-
-    def fill(dst, frame):
-        slot = slot_of(frame)
-        for yy in range(R):
-            dst[X * yy : X * yy + X, :] = KK[slot, yy]
 
     def fill_border(dst, frame):
         slot = slot_of(frame)
@@ -240,14 +248,22 @@
             dst[32 * side : 32 * side + 32, :] = EK[slot, side]
             dst[64 + 32 * side : 96 + 32 * side, :] = EF[side, frame]
 
+    slots = [slot_of(lax.rem(row + o, nrow)) for o in range(nrow)]
     msg_copies = []
-    for o in (2, 1, 3):
-        there = lax.rem(row + o, nrow)
-        fill(SB.at[o - 1], there)
-        cp = remote(SB.at[o - 1], RB.at[row], msend.at[o - 1], mrecv.at[o - 1], (tm, there, col))
-        cp.start()
-        msg_copies.append(cp)
-    fill(RB.at[row], row)
+    for k in range(NCH):
+        part = slice(X - (k + 1) * CH, X - k * CH)
+        ds = pl.ds(X - (k + 1) * CH, CH)
+        copies = []
+        for o in (2, 1, 3):
+            there = lax.rem(row + o, nrow)
+            SB[o - 1, :, part, :] = KK[slots[o], :, part, :]
+            cp = remote(
+                SB.at[o - 1, :, ds, :], RB.at[row, :, ds, :], msend.at[k, o - 1], mrecv.at[k, o - 1], (tm, there, col)
+            )
+            cp.start()
+            copies.append(cp)
+        msg_copies.append(copies)
+    RB[row] = KK[slots[0]]
 
     @pl.when(cross_right)
     def _():
@@ -272,90 +288,140 @@
     fill_border(RH.at[row], row)
 
     own_feat.wait()
-    for cp in feat_copies + msg_copies + border_copies:
+    for cp in feat_copies + border_copies:
         cp.wait_recv()
 
     hrow = lax.broadcasted_iota(jnp.int32, (64, C), 0)
     border = jnp.where(hrow < 32, has_left.astype(jnp.int32), has_right.astype(jnp.int32)) == 1
 
     def arrange(rs, carry):
-        kh = jnp.where(border, RH[rs, :64, :].astype(F32), 0.0).astype(BF)
+        kh = jnp.where(border, RH[rs, :64, :].astype(F32), 0.0)
         fh = jnp.where(border, RH[rs, 64:, :].astype(F32), 0.0)
         for yy in range(R):
             y = R * rs + yy
-            src = jnp.concatenate([RB[rs, X * yy : X * yy + X, :], kh], axis=0)
-            KR[y] = dot(PM[yy], src)
+            KR[y, 140:148, :] = kh[8 * yy : 8 * yy + 8]
+            KR[y, 4:12, :] = kh[32 + 8 * yy : 40 + 8 * yy]
             fr = jnp.concatenate(
                 [fh[8 * yy : 8 * yy + 8], F[rs, yy].astype(F32), fh[32 + 8 * yy : 40 + 8 * yy]], axis=0
             )
             FQ[y] = fr
             for j in range(3):
                 sh = fr if j == 1 else pltpu.roll(fr, (1 - j) % D, 0)
-                J3[y + 1, :, 256 * j + 128 : 256 * j + 256] = sh.astype(BF)
+                JF[y + 1, :, 128 * j : 128 * j + 128] = sh.astype(BF)
         return carry
 
     lax.fori_loop(0, NF, arrange, 0)
 
+    def pairs(src, first, gap):
+        return jnp.concatenate(
+            [
+                jnp.concatenate([src[first + t * (3 - gap)] for t in range(4)], axis=1),
+                jnp.concatenate([src[first + gap + t * (3 - gap)] for t in range(4)], axis=1),
+            ],
+            axis=0,
+        )
+
+    def joint_frames(p, carry):
+        HF[p] = dot(pairs(JF, 4 * p, 2), WF[...].reshape(1536, 256))
+        return carry
+
+    lax.fori_loop(0, H // 4, joint_frames, 0)
+
     scale = 1.0 / math.sqrt(C)
+    lane = lax.broadcasted_iota(jnp.int32, (8, 128), 1)
 
     def correlate(p, carry):
-        parts = []
+        parts = [[], []]
         for h in range(2):
             d0 = pl.multiple_of(16 * p + 8 * h, 8)
             e0 = pl.multiple_of(136 - 16 * p - 8 * h, 8)
             qs = FQ[:, pl.ds(d0, 8), :].reshape(H * 8, C).astype(BF)
             ks = KR[:, pl.ds(e0, 16), :].reshape(H * 16, C).astype(BF)
-            sc = dot_t(qs, ks).reshape(H, 8, 256) * scale
-            lo = pltpu.roll(sc[:, :, :128], 0, 2, stride=1, stride_axis=1)
-            hi = pltpu.roll(sc[:, :, 128:], 0, 2, stride=1, stride_axis=1)
-            parts.append(jnp.concatenate([lo, hi], axis=2))
+            sc = (dot_t(qs, ks) * scale).reshape(H, 8, 256)
+            for y in range(H):
+                turn = (64 - 16 * y) % 256
+                by = turn % 128
+                lo = pltpu.roll(sc[y, :, :128], by, 1, stride=1, stride_axis=0)
+                hi = pltpu.roll(sc[y, :, 128:], by, 1, stride=1, stride_axis=0)
+                if turn >= 128:
+                    lo, hi = hi, lo
+                low = jnp.where(lane < by, hi, lo) if by else lo
+                high = jnp.where(lane < by, lo, hi) if by else hi
+                if y < 4:
+                    low = jnp.where(lane >= 16 * (4 - y), low, 0.0)
+                if y > 11:
+                    high = jnp.zeros_like(high)
+                if y > 12:
+                    low = jnp.where(lane < 16 * (20 - y), low, 0.0)
+                parts[h].append(jnp.concatenate([low, high], axis=1))
         c0 = pl.multiple_of(16 * p, 16)
-        CB[:, pl.ds(c0, 16), :] = jnp.concatenate(parts, axis=1).astype(BF)
-        return carry
-
-    lax.fori_loop(0, D // 16, correlate, 0)
-
-    def motion(y, carry):
-        w0 = pl.multiple_of(16 * (15 - y), 16)
-        m = dot(CB[y], WB[pl.ds(w0, 256), :])
-        m = jnp.where(inside, jnp.maximum(m, 0.0), 0.0)
+        for y in range(H):
+            CB[y, pl.ds(c0, 16), :] = jnp.concatenate([parts[0][y], parts[1][y]], axis=0).astype(BF)
+        return carry
+
+    done = 0
+    for k in range(NCH):
+        for cp in msg_copies[k]:
+            cp.wait_recv()
+        s0 = X - (k + 1) * CH
+
+        def place(rs, carry, s0=s0):
+            y0 = R * rs
+            for yy in range(R):
+                KR[y0 + yy, 12 + s0 : 12 + s0 + CH, :] = RB[rs, yy, s0 : s0 + CH, :].astype(F32)
+            return carry
+
+        lax.fori_loop(0, NF, place, 0)
+        upto = D // 16 if k == NCH - 1 else ((k + 1) * CH - 12) // 16 + 1
+        lax.fori_loop(done, upto, correlate, 0)
+        n = 16 * (upto - done)
+        d0 = 16 * done
+        m = dot(CB[:, d0 : d0 + n, :].reshape(H * n, 256), WR[...]).reshape(H, n, C)
+        m = jnp.where(inside[d0 : d0 + n][None], jnp.maximum(m, 0.0), 0.0)
+        MF[:, d0 + 8 : d0 + 8 + n, :] = m
+        done = upto
+
+    def shifts(y, carry):
         for j in range(3):
-            sh = m if j == 1 else pltpu.roll(m, (1 - j) % D, 0)
-            J3[y + 1, :, 256 * j : 256 * j + 128] = sh.astype(BF)
-        return carry
-
-    lax.fori_loop(0, H, motion, 0)
+            JM[y + 1, :, 128 * j : 128 * j + 128] = MF[y, 7 + j : 7 + j + D, :].astype(BF)
+        return carry
+
+    lax.fori_loop(0, H, shifts, 0)
 
     def joint(p, carry):
-        lhs = jnp.concatenate([J3[2 * p + t] for t in range(4)], axis=1)
-        h = dot(lhs, W1[...].reshape(4 * 768, 256))
-        for o in range(2):
-            ho = jnp.where(inside, jnp.maximum(h[:, 128 * o : 128 * o + 128], 0.0), 0.0)
-            for j in range(3):
-                sh = ho if j == 1 else pltpu.roll(ho, (2 - 2 * j) % D, 0)
-                H3[2 * p + o + 2, :, 128 * j : 128 * j + 128] = sh.astype(BF)
-        return carry
-
-    lax.fori_loop(0, H // 2, joint, 0)
+        h = dot(pairs(JM, 4 * p, 2), WM[...].reshape(1536, 256)) + HF[p]
+        for u in range(2):
+            for o in range(2):
+                ho = h[D * u : D * u + D, 128 * o : 128 * o + 128]
+                ho = jnp.where(inside, jnp.maximum(ho, 0.0), 0.0)
+                for j in range(3):
+                    sh = ho if j == 1 else pltpu.roll(ho, (2 - 2 * j) % D, 0)
+                    H3[4 * p + 2 * u + o + 2, :, 128 * j : 128 * j + 128] = sh.astype(BF)
+        return carry
+
+    lax.fori_loop(0, H // 4, joint, 0)
 
     def dilated(p, carry):
-        y0 = 4 * (p // 2) + lax.rem(p, 2)
-        lhs = jnp.concatenate([H3[y0 + 2 * t] for t in range(4)], axis=1)
-        h = dot(lhs, W2[...].reshape(4 * 384, 256))
-        for o in range(2):
-            ho = jnp.where(inside, jnp.maximum(h[:, 128 * o : 128 * o + 128], 0.0), 0.0)
-            for j in range(3):
-                sh = pltpu.roll(ho, (-7 - j) % D, 0)[:X]
-                HB[y0 + 2 * o + 1, :, 128 * j : 128 * j + 128] = sh.astype(BF)
-        return carry
-
-    lax.fori_loop(0, H // 2, dilated, 0)
+        h = dot(pairs(H3, 4 * p, 1), W2[...].reshape(1536, 256))
+        rows = []
+        for yy in range(R):
+            u, o = yy % 2, yy // 2
+            ho = h[D * u : D * u + D, 128 * o : 128 * o + 128]
+            ho = jnp.where(inside, jnp.maximum(ho, 0.0), 0.0)
+            rows.append(
+                jnp.concatenate([pltpu.roll(ho, (-7 - j) % D, 0)[:X].astype(BF) for j in range(3)], axis=1)
+            )
+        res = dot_t(W4[...].astype(BF), jnp.concatenate(rows, axis=0))
+        for yy in range(R):
+            RS[R * p + yy + 1] = res[:, X * yy : X * yy + X]
+        return carry
+
+    lax.fori_loop(0, NF, dilated, 0)
 
     def head(rr, carry):
         for yy in range(R):
             y = R * rr + yy
-            rhs = jnp.concatenate([HB[y + i] for i in range(3)], axis=1)
-            res = dot_t(FW[...], rhs)
+            res = RS[y, 0:2, :] + RS[y + 1, 2:4, :] + RS[y + 2, 4:6, :]
             OS[rr, :, yy : yy + 1, :] = res.reshape(2, 1, X)
         return carry
 
@@ -372,7 +438,7 @@
         cp.wait_recv()
     out[...] = RO[...]
 
-    for cp in feat_copies + msg_copies + border_copies + out_copies:
+    for cp in feat_copies + sum(msg_copies, []) + border_copies + out_copies:
         cp.wait_send()
     for side, has in ((0, has_left), (1, has_right)):
 
@@ -405,39 +471,44 @@
             scratch_shapes=[
                 pltpu.VMEM((NF, R, X, C), BF),
                 pltpu.VMEM((2, R, X, C), BF),
+                pltpu.VMEM((R, X, C), BF),
                 pltpu.VMEM((2, NF, R, 16, C), BF),
                 pltpu.VMEM((2, R * 8, C), BF),
                 pltpu.VMEM((2, NF, R * 8, C), BF),
                 pltpu.VMEM((2, 2, R * 8, C), BF),
                 pltpu.VMEM((2, NF, R * 8, C), BF),
-                pltpu.VMEM((3, MSG, C), BF),
-                pltpu.VMEM((NF, MSG, C), BF),
+                pltpu.VMEM((3, R, X, C), BF),
+                pltpu.VMEM((NF, R, X, C), BF),
                 pltpu.VMEM((3, 128, C), BF),
                 pltpu.VMEM((NF, 128, C), BF),
                 pltpu.VMEM((81, C), BF),
                 pltpu.VMEM((2, 9 * C), BF),
-                pltpu.VMEM((R, E, 192), BF),
                 pltpu.VMEM((H, D, C), F32),
                 pltpu.VMEM((H, E, C), F32),
                 pltpu.VMEM((H, D, 256), BF),
-                pltpu.VMEM((31 * 16, C), BF),
-                pltpu.VMEM((H + 2, D, 768), BF),
-                pltpu.VMEM((4, 768, 256), BF),
+                pltpu.VMEM((256, C), BF),
+                pltpu.VMEM((H, D + 16, C), F32),
+                pltpu.VMEM((H + 2, D, 384), BF),
+                pltpu.VMEM((H + 2, D, 384), BF),
+                pltpu.VMEM((4, 3, C, 256), BF),
+                pltpu.VMEM((4, 3, C, 256), BF),
+                pltpu.VMEM((H // 4, 2 * D, 256), F32),
                 pltpu.VMEM((H + 4, D, 384), BF),
                 pltpu.VMEM((4, 384, 256), BF),
-                pltpu.VMEM((H + 2, X, 384), BF),
+                pltpu.VMEM((8, 384), F32),
+                pltpu.VMEM((H + 2, 8, X), F32),
                 pltpu.VMEM((NF, 2, R, X), F32),
                 pltpu.VMEM((NF, 2, R, X), F32),
                 dma((6,)),
-                dma((2, 3, 2)),
+                dma((3, 3, 2)),
                 dma,
                 dma,
                 dma((2, 3)),
                 dma((2, 3)),
                 dma((3,)),
                 dma((3,)),
-                dma((3,)),
-                dma((3,)),
+                dma((NCH, 3)),
+                dma((NCH, 3)),
                 dma((3,)),
                 dma((3,)),
                 pltpu.SemaphoreType.REGULAR,
@@ -452,7 +523,7 @@
             feat,
             keys,
             mw,
-            jw.reshape(3, 768, 128),
+            jw,
             dw.reshape(3, 384, 128),
             fw.reshape(2, 1152),
         )

time: 42 us -> 38.4 us (0.914)
  the two profiles are of different devices: /device:TPU:1 before, /device:TPU:2 now
where the time goes in v3:
time: 38.4 us; the launch traced here: 38.3 us
  Pallas kernels  36.9 us (96%)
  local copies, waits for them, and re-layouts  1.32 us (3%)
    pallas_call x1, Pallas kernels, step(): pl.pallas_call(functools.partial(kernel, ntm, ncol), out_shape=jax.ShapeD...  36.9 us
    unnamed x1, local copies, waits for them, and re-layouts  1.32 us

profile of v3, /device:TPU:2, one launch (start us, length us, event | category | flops | bytes accessed | tf_op | source)
XLA Modules:
  0.0 38.3 jit_solution(11439258874008931139)
XLA Ops:
  0.0 36.9 %shard_map.73 = f32[4,2,4,128]{3,2,1,0:T(4,128)} custom-call(s32[4]{0:T(128)} %bitcast.5, bf16[4,4,128,128]{3,2,1,0:T(8,128)(2,1)} %feat.1, bf16[1,4,128,128]{3,2,1,0:T(8,128)(2,1)} %keys.1, bf16[81,128]{1,0:T(8,128)(2,1)} %mw.1, bf16[3,3,256,128]{3,2,1,0:T(8,128)(2,1)} %jw.1, bf16[3,384,128]{2,1,0:T(8,128)(2,1)} %bitcast.3, bf16[2,1152]{1,0:T(2,128)(2,1)} %bitcast.4), custom_call_target="tpu_custom_call" | custom-call | tf_op jit(solution)/shard_map/pallas_call | solution.py:458
  36.9 1.3 %copy.11 = f32[4,2,4,128]{3,2,1,0:T(4,128)} copy(f32[4,2,4,128]{3,2,1,0:T(4,128)} %shard_map.73) | data formatting | bytes 32768

commit v4 on v3

--- a/solution.py
+++ b/solution.py
@@ -48,7 +48,8 @@
     FE,
     ES_K,
     ES_F,
-    EK,
+    EKL,
+    EKR,
     EF,
     SB,
     RB,
@@ -69,9 +70,9 @@
     H3,
     W2,
     W4,
+    HB,
     RS,
     OS,
-    RO,
     loc_sem,
     w_sem,
     ksend,
@@ -88,6 +89,7 @@
     hsend,
     hrecv,
 ):
+    EK = (EKL, EKR)
     tm = lax.axis_index("tm")
     row = lax.axis_index("row")
     col = lax.axis_index("col")
@@ -177,16 +179,16 @@
         other = 1 - side
         c = col + 2 * side - 1
         return [
-            remote(ES_K.at[side], EK.at[0, other], esend.at[side, 0], erecv.at[other, 0], (tm_next, row, c)),
-            remote(ES_K.at[side], EK.at[1, other], esend.at[side, 1], erecv.at[other, 1], (tm, row, c)),
+            remote(ES_K.at[side], EK[other].at[0], esend.at[side, 0], erecv.at[other, 0], (tm_next, row, c)),
+            remote(ES_K.at[side], EK[other].at[1], esend.at[side, 1], erecv.at[other, 1], (tm, row, c)),
             remote(ES_F.at[side], EF.at[other], esend.at[side, 2], erecv.at[other, 2], (tm, row, c)),
         ]
 
     def edge_waits(side):
         c = col + 2 * side - 1
         return [
-            remote(ES_K.at[side], EK.at[0, side], esend.at[side, 0], erecv.at[side, 0], (tm_next, row, c)),
-            remote(ES_K.at[side], EK.at[1, side], esend.at[side, 1], erecv.at[side, 1], (tm, row, c)),
+            remote(ES_K.at[side], EK[side].at[0], esend.at[side, 0], erecv.at[side, 0], (tm_next, row, c)),
+            remote(ES_K.at[side], EK[side].at[1], esend.at[side, 1], erecv.at[side, 1], (tm, row, c)),
             remote(ES_F.at[side], EF.at[side], esend.at[side, 2], erecv.at[side, 2], (tm, row, c)),
         ]
 
@@ -220,9 +222,10 @@
         w[3, :, :, 0:128] = zero
     W2[0, :, 128:256] = zero.reshape(384, 128)
     W2[3, :, 0:128] = zero.reshape(384, 128)
-    for i in range(3):
-        W4[2 * i : 2 * i + 2, :] = FW[:, 384 * i : 384 * i + 384].astype(F32)
-    W4[6:8, :] = jnp.zeros((2, 384), F32)
+    W4[...] = jnp.zeros_like(W4)
+    for j in range(3):
+        for i in range(3):
+            W4[8 * j + 2 * i : 8 * j + 2 * i + 2, :] = FW[:, 384 * i + 128 * j : 384 * i + 128 * j + 128].astype(F32)
     for i in (0, H + 1):
         JF[i] = jnp.zeros((D, 384), BF)
         JM[i] = jnp.zeros((D, 384), BF)
@@ -237,20 +240,54 @@
     dd = lax.broadcasted_iota(jnp.int32, (D, C), 0)
     inside = (has_left | (dd >= 8)) & (has_right | (dd < X + 8))
 
+    slots = [
+        jnp.where(kidx[lax.rem(row + o, nrow)] == tm, 1, 0) for o in range(nrow)
+    ]
+
+    def border_copies(side):
+        return [
+            remote(
+                SH.at[side, o - 1],
+                RH.at[row, side],
+                hsend.at[side, o - 1],
+                hrecv.at[side, o - 1],
+                (tm, lax.rem(row + o, nrow), col),
+            )
+            for o in (2, 1, 3)
+        ]
+
+    def fill_border(dst, o, side):
+        dst[0:32, :] = EK[side][slots[o]]
+        dst[32:64, :] = EF[side, lax.rem(row + o, nrow)]
+
+    def pass_border(side):
+        for cp in edge_waits(side):
+            cp.wait_recv()
+        for o, cp in zip((2, 1, 3), border_copies(side)):
+            fill_border(SH.at[side, o - 1], o, side)
+            cp.start()
+        fill_border(RH.at[row, side], 0, side)
+
+    @pl.when(has_left)
+    def _():
+        pass_border(0)
+
+    @pl.when(near_right)
+    def _():
+        pass_border(1)
+
     key_copy.wait()
-
-    def slot_of(frame):
-        return jnp.where(kidx[frame] == tm, 1, 0)
-
-    def fill_border(dst, frame):
-        slot = slot_of(frame)
-        for side in range(2):
-            dst[32 * side : 32 * side + 32, :] = EK[slot, side]
-            dst[64 + 32 * side : 96 + 32 * side, :] = EF[side, frame]
-
-    slots = [slot_of(lax.rem(row + o, nrow)) for o in range(nrow)]
     msg_copies = []
     for k in range(NCH):
+        if k == NCH // 2:
+
+            @pl.when(cross_right)
+            def _():
+                pl.semaphore_wait(ready, 2)
+                for cp in edge_copies(1):
+                    cp.start()
+                pass_border(1)
+
         part = slice(X - (k + 1) * CH, X - k * CH)
         ds = pl.ds(X - (k + 1) * CH, CH)
         copies = []
@@ -265,45 +302,26 @@
         msg_copies.append(copies)
     RB[row] = KK[slots[0]]
 
-    @pl.when(cross_right)
-    def _():
-        pl.semaphore_wait(ready, 2)
-        for cp in edge_copies(1):
-            cp.start()
-
+    own_feat.wait()
+    for cp in feat_copies:
+        cp.wait_recv()
     for side, has in ((0, has_left), (1, has_right)):
 
         @pl.when(has)
         def _(side=side):
-            for cp in edge_waits(side):
+            for cp in border_copies(side):
                 cp.wait_recv()
 
-    border_copies = []
-    for o in (2, 1, 3):
-        there = lax.rem(row + o, nrow)
-        fill_border(SH.at[o - 1], there)
-        cp = remote(SH.at[o - 1], RH.at[row], hsend.at[o - 1], hrecv.at[o - 1], (tm, there, col))
-        cp.start()
-        border_copies.append(cp)
-    fill_border(RH.at[row], row)
-
-    own_feat.wait()
-    for cp in feat_copies + border_copies:
-        cp.wait_recv()
-
-    hrow = lax.broadcasted_iota(jnp.int32, (64, C), 0)
-    border = jnp.where(hrow < 32, has_left.astype(jnp.int32), has_right.astype(jnp.int32)) == 1
 
     def arrange(rs, carry):
-        kh = jnp.where(border, RH[rs, :64, :].astype(F32), 0.0)
-        fh = jnp.where(border, RH[rs, 64:, :].astype(F32), 0.0)
+        left = jnp.where(has_left, RH[rs, 0].astype(F32), 0.0)
+        right = jnp.where(has_right, RH[rs, 1].astype(F32), 0.0)
         for yy in range(R):
             y = R * rs + yy
-            KR[y, 140:148, :] = kh[8 * yy : 8 * yy + 8]
-            KR[y, 4:12, :] = kh[32 + 8 * yy : 40 + 8 * yy]
-            fr = jnp.concatenate(
-                [fh[8 * yy : 8 * yy + 8], F[rs, yy].astype(F32), fh[32 + 8 * yy : 40 + 8 * yy]], axis=0
-            )
+            b = 8 * yy
+            KR[y, 140:148, :] = left[b : b + 8]
+            KR[y, 4:12, :] = right[b : b + 8]
+            fr = jnp.concatenate([left[32 + b : 40 + b], F[rs, yy].astype(F32), right[32 + b : 40 + b]], axis=0)
             FQ[y] = fr
             for j in range(3):
                 sh = fr if j == 1 else pltpu.roll(fr, (1 - j) % D, 0)
@@ -360,6 +378,7 @@
         return carry
 
     done = 0
+    shifted = 0
     for k in range(NCH):
         for cp in msg_copies[k]:
             cp.wait_recv()
@@ -380,13 +399,15 @@
         m = jnp.where(inside[d0 : d0 + n][None], jnp.maximum(m, 0.0), 0.0)
         MF[:, d0 + 8 : d0 + 8 + n, :] = m
         done = upto
-
-    def shifts(y, carry):
-        for j in range(3):
-            JM[y + 1, :, 128 * j : 128 * j + 128] = MF[y, 7 + j : 7 + j + D, :].astype(BF)
-        return carry
-
-    lax.fori_loop(0, H, shifts, 0)
+        d1 = D if k == NCH - 1 else 16 * done - 16
+
+        def shifts(y, carry, d0=shifted, d1=d1):
+            for j in range(3):
+                JM[y + 1, d0:d1, 128 * j : 128 * j + 128] = MF[y, 7 + j + d0 : 7 + j + d1, :].astype(BF)
+            return carry
+
+        lax.fori_loop(0, H, shifts, 0)
+        shifted = d1
 
     def joint(p, carry):
         h = dot(pairs(JM, 4 * p, 2), WM[...].reshape(1536, 256)) + HF[p]
@@ -399,24 +420,27 @@
                     H3[4 * p + 2 * u + o + 2, :, 128 * j : 128 * j + 128] = sh.astype(BF)
         return carry
 
-    lax.fori_loop(0, H // 4, joint, 0)
+    lax.fori_loop(0, H // 4, joint, 0, unroll=True)
 
     def dilated(p, carry):
         h = dot(pairs(H3, 4 * p, 1), W2[...].reshape(1536, 256))
-        rows = []
         for yy in range(R):
             u, o = yy % 2, yy // 2
             ho = h[D * u : D * u + D, 128 * o : 128 * o + 128]
-            ho = jnp.where(inside, jnp.maximum(ho, 0.0), 0.0)
-            rows.append(
-                jnp.concatenate([pltpu.roll(ho, (-7 - j) % D, 0)[:X].astype(BF) for j in range(3)], axis=1)
+            HB[R * p + yy] = jnp.where(inside, jnp.maximum(ho, 0.0), 0.0).astype(BF)
+        return carry
+
+    lax.fori_loop(0, NF, dilated, 0, unroll=True)
+
+    def taps(p, carry):
+        res = dot_t(W4[...].astype(BF), HB[pl.ds(R * p, R)].reshape(R * D, C))
+        for yy in range(R):
+            RS[R * p + yy + 1] = sum(
+                res[8 * j : 8 * j + 8, D * yy + 7 + j : D * yy + 7 + j + X] for j in range(3)
             )
-        res = dot_t(W4[...].astype(BF), jnp.concatenate(rows, axis=0))
-        for yy in range(R):
-            RS[R * p + yy + 1] = res[:, X * yy : X * yy + X]
-        return carry
-
-    lax.fori_loop(0, NF, dilated, 0)
+        return carry
+
+    lax.fori_loop(0, NF, taps, 0, unroll=True)
 
     def head(rr, carry):
         for yy in range(R):
@@ -425,26 +449,26 @@
             OS[rr, :, yy : yy + 1, :] = res.reshape(2, 1, X)
         return carry
 
-    lax.fori_loop(0, NF, head, 0)
+    lax.fori_loop(0, NF, head, 0, unroll=True)
 
     out_copies = []
     for o in range(1, nrow):
         there = lax.rem(row + o, nrow)
-        cp = remote(OS.at[there], RO.at[row], osend.at[o - 1], orecv.at[o - 1], (tm, there, col))
+        cp = remote(OS.at[there], out.at[row], osend.at[o - 1], orecv.at[o - 1], (tm, there, col))
         cp.start()
         out_copies.append(cp)
-    RO[row] = OS[row]
+    own_out = local(OS.at[row], out.at[row], loc_sem.at[6])
+    own_out.wait()
     for cp in out_copies:
         cp.wait_recv()
-    out[...] = RO[...]
-
-    for cp in feat_copies + sum(msg_copies, []) + border_copies + out_copies:
+
+    for cp in feat_copies + sum(msg_copies, []) + out_copies:
         cp.wait_send()
     for side, has in ((0, has_left), (1, has_right)):
 
         @pl.when(has)
         def _(side=side):
-            for cp in edge_copies(side):
+            for cp in edge_copies(side) + border_copies(side):
                 cp.wait_send()
 
 
@@ -453,7 +477,6 @@
 
     def step(feat, keys, kidx, mw, jw, dw, fw):
         anyspec = pl.BlockSpec(memory_space=pltpu.HBM)
-        vspec = pl.BlockSpec(memory_space=pltpu.VMEM)
         dma = pltpu.SemaphoreType.DMA
         return pl.pallas_call(
             functools.partial(kernel, ntm, ncol),
@@ -467,7 +490,7 @@
                 anyspec,
                 anyspec,
             ],
-            out_specs=vspec,
+            out_specs=anyspec,
             scratch_shapes=[
                 pltpu.VMEM((NF, R, X, C), BF),
                 pltpu.VMEM((2, R, X, C), BF),
@@ -475,12 +498,13 @@
                 pltpu.VMEM((2, NF, R, 16, C), BF),
                 pltpu.VMEM((2, R * 8, C), BF),
                 pltpu.VMEM((2, NF, R * 8, C), BF),
-                pltpu.VMEM((2, 2, R * 8, C), BF),
+                pltpu.VMEM((2, R * 8, C), BF),
+                pltpu.VMEM((2, R * 8, C), BF),
                 pltpu.VMEM((2, NF, R * 8, C), BF),
                 pltpu.VMEM((3, R, X, C), BF),
                 pltpu.VMEM((NF, R, X, C), BF),
-                pltpu.VMEM((3, 128, C), BF),
-                pltpu.VMEM((NF, 128, C), BF),
+                pltpu.VMEM((2, 3, 64, C), BF),
+                pltpu.VMEM((NF, 2, 64, C), BF),
                 pltpu.VMEM((81, C), BF),
                 pltpu.VMEM((2, 9 * C), BF),
                 pltpu.VMEM((H, D, C), F32),
@@ -495,11 +519,11 @@
                 pltpu.VMEM((H // 4, 2 * D, 256), F32),
                 pltpu.VMEM((H + 4, D, 384), BF),
                 pltpu.VMEM((4, 384, 256), BF),
-                pltpu.VMEM((8, 384), F32),
+                pltpu.VMEM((24, C), F32),
+                pltpu.VMEM((H, D, C), BF),
                 pltpu.VMEM((H + 2, 8, X), F32),
                 pltpu.VMEM((NF, 2, R, X), F32),
-                pltpu.VMEM((NF, 2, R, X), F32),
-                dma((6,)),
+                dma((7,)),
                 dma((3, 3, 2)),
                 dma,
                 dma,
@@ -512,8 +536,8 @@
                 dma((3,)),
                 dma((3,)),
                 pltpu.SemaphoreType.REGULAR,
-                dma((3,)),
-                dma((3,)),
+                dma((2, 3)),
+                dma((2, 3)),
             ],
             compiler_params=pltpu.CompilerParams(
                 collective_id=0, has_side_effects=True, vmem_limit_bytes=60 * 1024 * 1024

time: 38.4 us -> 31.8 us (0.83)
  the two profiles are of different devices: /device:TPU:2 before, /device:TPU:1 now
where the time goes in v4:
time: 31.8 us; the launch traced here: 31.4 us
  Pallas kernels  30.1 us (95%)
  local copies, waits for them, and re-layouts  1.32 us (4%)
    pallas_call x1, Pallas kernels, step(): pl.pallas_call(functools.partial(kernel, ntm, ncol), out_shape=jax.ShapeD...  30.1 us
    unnamed x1, local copies, waits for them, and re-layouts  1.32 us

profile of v4, /device:TPU:1, one launch (start us, length us, event | category | flops | bytes accessed | tf_op | source)
XLA Modules:
  0.0 31.4 jit_solution(9364032422115602564)
XLA Ops:
  0.0 30.1 %shard_map.73 = f32[4,2,4,128]{3,2,1,0:T(4,128)} custom-call(s32[4]{0:T(128)} %bitcast.5, bf16[4,4,128,128]{3,2,1,0:T(8,128)(2,1)} %feat.1, bf16[1,4,128,128]{3,2,1,0:T(8,128)(2,1)} %keys.1, bf16[81,128]{1,0:T(8,128)(2,1)} %mw.1, bf16[3,3,256,128]{3,2,1,0:T(8,128)(2,1)} %jw.1, bf16[3,384,128]{2,1,0:T(8,128)(2,1)} %bitcast.3, bf16[2,1152]{1,0:T(2,128)(2,1)} %bitcast.4), custom_call_target="tpu_custom_call" | custom-call | tf_op jit(solution)/shard_map/pallas_call | solution.py:481
  30.1 1.3 %copy.11 = f32[4,2,4,128]{3,2,1,0:T(4,128)} copy(f32[4,2,4,128]{3,2,1,0:T(4,128)} %shard_map.73) | data formatting | bytes 32768

commit v5 on v4

--- a/solution.py
+++ b/solution.py
@@ -96,6 +96,8 @@
     nrow = NF
     tm_next = lax.rem(tm + 1, ntm)
     tm_prev = lax.rem(tm + ntm - 1, ntm)
+    has_next = tm < ntm - 1
+    has_prev = tm > 0
     has_left = col > 0
     has_right = col < ncol - 1
 
@@ -192,15 +194,27 @@
             remote(ES_F.at[side], EF.at[side], esend.at[side, 2], erecv.at[side, 2], (tm, row, c)),
         ]
 
+    def start_edges(side):
+        to_next, *others = edge_copies(side)
+        for cp in others:
+            cp.start()
+
+        @pl.when(has_next)
+        def _():
+            to_next.start()
+
     for side, go in ((0, has_left), (1, near_right)):
 
         @pl.when(go)
         def _(side=side):
-            for cp in edge_copies(side):
-                cp.start()
+            start_edges(side)
 
     key_copy = remote(KK.at[1], KK.at[0], ksend, krecv, (tm_next, row, col))
-    key_copy.start()
+
+    @pl.when(has_next)
+    def _():
+        key_copy.start()
+
     feat_copies = []
     for o in (2, 1, 3):
         there = lax.rem(row + o, nrow)
@@ -261,14 +275,20 @@
         dst[32:64, :] = EF[side, lax.rem(row + o, nrow)]
 
     def pass_border(side):
-        for cp in edge_waits(side):
+        from_prev, *others = edge_waits(side)
+        for cp in others:
             cp.wait_recv()
+
+        @pl.when(has_prev)
+        def _():
+            from_prev.wait_recv()
+
         for o, cp in zip((2, 1, 3), border_copies(side)):
             fill_border(SH.at[side, o - 1], o, side)
             cp.start()
         fill_border(RH.at[row, side], 0, side)
 
-    @pl.when(has_left)
+    @pl.when(near_left)
     def _():
         pass_border(0)
 
@@ -276,16 +296,34 @@
     def _():
         pass_border(1)
 
-    key_copy.wait()
+
+    @pl.when(has_next)
+    def _():
+        key_copy.wait_send()
+
+    @pl.when(has_prev)
+    def _():
+        key_copy.wait_recv()
+
     msg_copies = []
     for k in range(NCH):
-        if k == NCH // 2:
+        if k == 1:
+
+            @pl.when(cross_left)
+            def _():
+                pass_border(0)
+
+        if k == 2:
 
             @pl.when(cross_right)
             def _():
                 pl.semaphore_wait(ready, 2)
-                for cp in edge_copies(1):
-                    cp.start()
+                start_edges(1)
+
+        if k == 3:
+
+            @pl.when(cross_right)
+            def _():
                 pass_border(1)
 
         part = slice(X - (k + 1) * CH, X - k * CH)
@@ -305,23 +343,12 @@
     own_feat.wait()
     for cp in feat_copies:
         cp.wait_recv()
-    for side, has in ((0, has_left), (1, has_right)):
-
-        @pl.when(has)
-        def _(side=side):
-            for cp in border_copies(side):
-                cp.wait_recv()
-
+    edge = jnp.zeros((8, C), F32)
 
     def arrange(rs, carry):
-        left = jnp.where(has_left, RH[rs, 0].astype(F32), 0.0)
-        right = jnp.where(has_right, RH[rs, 1].astype(F32), 0.0)
         for yy in range(R):
             y = R * rs + yy
-            b = 8 * yy
-            KR[y, 140:148, :] = left[b : b + 8]
-            KR[y, 4:12, :] = right[b : b + 8]
-            fr = jnp.concatenate([left[32 + b : 40 + b], F[rs, yy].astype(F32), right[32 + b : 40 + b]], axis=0)
+            fr = jnp.concatenate([edge, F[rs, yy].astype(F32), edge], axis=0)
             FQ[y] = fr
             for j in range(3):
                 sh = fr if j == 1 else pltpu.roll(fr, (1 - j) % D, 0)
@@ -377,9 +404,69 @@
             CB[y, pl.ds(c0, 16), :] = jnp.concatenate([parts[0][y], parts[1][y]], axis=0).astype(BF)
         return carry
 
-    done = 0
-    shifted = 0
+    def motion(corr, keep):
+        n = corr.shape[1]
+        m = dot(corr.reshape(H * n, 256), WR[...]).reshape(H, n, C)
+        return jnp.where(keep[None], jnp.maximum(m, 0.0), 0.0)
+
+    def shift(d0, d1):
+        def shifts(y, carry):
+            for j in range(3):
+                JM[y + 1, d0:d1, 128 * j : 128 * j + 128] = MF[y, 7 + j + d0 : 7 + j + d1, :].astype(BF)
+            return carry
+
+        lax.fori_loop(0, H, shifts, 0)
+
+    def amend(rs, carry):
+        left = jnp.where(has_left, RH[rs, 0].astype(F32), 0.0)
+        right = jnp.where(has_right, RH[rs, 1].astype(F32), 0.0)
+        for yy in range(R):
+            y = R * rs + yy
+            b = 8 * yy
+            KR[y, 140:148, :] = left[b : b + 8]
+            KR[y, 4:12, :] = right[b : b + 8]
+            lf, rf = left[32 + b : 40 + b], right[32 + b : 40 + b]
+            FQ[y, 0:8, :] = lf
+            FQ[y, D - 8 : D, :] = rf
+            ends = (
+                jnp.concatenate([lf, F[rs, yy, 0:16, :].astype(F32)], axis=0),
+                jnp.concatenate([F[rs, yy, X - 16 :, :].astype(F32), rf], axis=0),
+            )
+            for side, at in ((0, 0), (1, D - 16)):
+                for j in range(3):
+                    sh = ends[side] if j == 1 else pltpu.roll(ends[side], (1 - j) % 24, 0)
+                    JF[y + 1, at : at + 16, 128 * j : 128 * j + 128] = sh[8 * side : 8 * side + 16].astype(BF)
+        return carry
+
+    done = 1
+    shifted = 32
     for k in range(NCH):
+        if k == NCH - 1:
+            for side, has in ((0, has_left), (1, has_right)):
+
+                @pl.when(has)
+                def _(side=side):
+                    for cp in border_copies(side):
+                        cp.wait_recv()
+
+            lax.fori_loop(0, NF, amend, 0)
+
+            spots = [(p, u, at) for p in range(H // 4) for u in range(2) for at in (0, D - 16)]
+            lhs = jnp.concatenate(
+                [
+                    jnp.concatenate([JF[4 * p + 2 * u + t, at : at + 16, :] for t in range(4)], axis=1)
+                    for p, u, at in spots
+                ],
+                axis=0,
+            )
+            hf = dot(lhs, WF[...].reshape(1536, 256))
+            for i, (p, u, at) in enumerate(spots):
+                HF[p, D * u + at : D * u + at + 16, :] = hf[16 * i : 16 * i + 16]
+
+            correlate(0, 0)
+            MF[:, 8:24, :] = motion(CB[:, 0:16, :], inside[0:16])
+            shift(0, 32)
+
         for cp in msg_copies[k]:
             cp.wait_recv()
         s0 = X - (k + 1) * CH
@@ -393,21 +480,13 @@
         lax.fori_loop(0, NF, place, 0)
         upto = D // 16 if k == NCH - 1 else ((k + 1) * CH - 12) // 16 + 1
         lax.fori_loop(done, upto, correlate, 0)
-        n = 16 * (upto - done)
-        d0 = 16 * done
-        m = dot(CB[:, d0 : d0 + n, :].reshape(H * n, 256), WR[...]).reshape(H, n, C)
-        m = jnp.where(inside[d0 : d0 + n][None], jnp.maximum(m, 0.0), 0.0)
-        MF[:, d0 + 8 : d0 + 8 + n, :] = m
+        d0, d1 = 16 * done, 16 * upto
+        MF[:, d0 + 8 : d1 + 8, :] = motion(CB[:, d0:d1, :], inside[d0:d1])
         done = upto
-        d1 = D if k == NCH - 1 else 16 * done - 16
-
-        def shifts(y, carry, d0=shifted, d1=d1):
-            for j in range(3):
-                JM[y + 1, d0:d1, 128 * j : 128 * j + 128] = MF[y, 7 + j + d0 : 7 + j + d1, :].astype(BF)
-            return carry
-
-        lax.fori_loop(0, H, shifts, 0)
-        shifted = d1
+        d1 = D if k == NCH - 1 else d1 - 16
+        if d1 > shifted:
+            shift(shifted, d1)
+            shifted = d1
 
     def joint(p, carry):
         h = dot(pairs(JM, 4 * p, 2), WM[...].reshape(1536, 256)) + HF[p]
@@ -468,8 +547,13 @@
 
         @pl.when(has)
         def _(side=side):
-            for cp in edge_copies(side) + border_copies(side):
+            to_next, *others = edge_copies(side)
+            for cp in others + border_copies(side):
                 cp.wait_send()
+
+            @pl.when(has_next)
+            def _():
+                to_next.wait_send()
 
 
 def solution(mesh):

time: 31.8 us -> 30.3 us (0.953)
  the two profiles are of different devices: /device:TPU:1 before, /device:TPU:224 now
where the time goes in v5:
time: 30.3 us; the launch traced here: 30.2 us
  Pallas kernels  28.8 us (95%)
  local copies, waits for them, and re-layouts  1.32 us (4%)
    pallas_call x1, Pallas kernels, step(): pl.pallas_call(functools.partial(kernel, ntm, ncol), out_shape=jax.ShapeD...  28.8 us
    unnamed x1, local copies, waits for them, and re-layouts  1.32 us

profile of v5, /device:TPU:224, one launch (start us, length us, event | category | flops | bytes accessed | tf_op | source)
XLA Modules:
  0.0 30.2 jit_solution(12472484302224741846)
XLA Ops:
  0.0 28.8 %shard_map.73 = f32[4,2,4,128]{3,2,1,0:T(4,128)} custom-call(s32[4]{0:T(128)} %bitcast.5, bf16[4,4,128,128]{3,2,1,0:T(8,128)(2,1)} %feat.1, bf16[1,4,128,128]{3,2,1,0:T(8,128)(2,1)} %keys.1, bf16[81,128]{1,0:T(8,128)(2,1)} %mw.1, bf16[3,3,256,128]{3,2,1,0:T(8,128)(2,1)} %jw.1, bf16[3,384,128]{2,1,0:T(8,128)(2,1)} %bitcast.3, bf16[2,1152]{1,0:T(2,128)(2,1)} %bitcast.4), custom_call_target="tpu_custom_call" | custom-call | tf_op jit(solution)/shard_map/pallas_call | solution.py:565
  28.8 1.3 %copy.11 = f32[4,2,4,128]{3,2,1,0:T(4,128)} copy(f32[4,2,4,128]{3,2,1,0:T(4,128)} %shard_map.73) | data formatting | bytes 32768

commit v6 on v5

--- a/solution.py
+++ b/solution.py
@@ -19,6 +19,7 @@
 H = NF * R
 D = X + 16
 E = X + 32
+PLAN = (((0, 1, 2), (0, 1)), ((3,), (2, 3)))
 NCH = 4
 CH = X // NCH
 
@@ -415,7 +416,7 @@
                 JM[y + 1, d0:d1, 128 * j : 128 * j + 128] = MF[y, 7 + j + d0 : 7 + j + d1, :].astype(BF)
             return carry
 
-        lax.fori_loop(0, H, shifts, 0)
+        lax.fori_loop(0, H, shifts, 0, unroll=True)
 
     def amend(rs, carry):
         left = jnp.where(has_left, RH[rs, 0].astype(F32), 0.0)
@@ -477,9 +478,9 @@
                 KR[y0 + yy, 12 + s0 : 12 + s0 + CH, :] = RB[rs, yy, s0 : s0 + CH, :].astype(F32)
             return carry
 
-        lax.fori_loop(0, NF, place, 0)
+        lax.fori_loop(0, NF, place, 0, unroll=True)
         upto = D // 16 if k == NCH - 1 else ((k + 1) * CH - 12) // 16 + 1
-        lax.fori_loop(done, upto, correlate, 0)
+        lax.fori_loop(done, upto, correlate, 0, unroll=k == NCH - 1)
         d0, d1 = 16 * done, 16 * upto
         MF[:, d0 + 8 : d1 + 8, :] = motion(CB[:, d0:d1, :], inside[d0:d1])
         done = upto
@@ -509,8 +510,6 @@
             HB[R * p + yy] = jnp.where(inside, jnp.maximum(ho, 0.0), 0.0).astype(BF)
         return carry
 
-    lax.fori_loop(0, NF, dilated, 0, unroll=True)
-
     def taps(p, carry):
         res = dot_t(W4[...].astype(BF), HB[pl.ds(R * p, R)].reshape(R * D, C))
         for yy in range(R):
@@ -519,8 +518,6 @@
             )
         return carry
 
-    lax.fori_loop(0, NF, taps, 0, unroll=True)
-
     def head(rr, carry):
         for yy in range(R):
             y = R * rr + yy
@@ -528,15 +525,38 @@
             OS[rr, :, yy : yy + 1, :] = res.reshape(2, 1, X)
         return carry
 
-    lax.fori_loop(0, NF, head, 0, unroll=True)
-
-    out_copies = []
-    for o in range(1, nrow):
-        there = lax.rem(row + o, nrow)
-        cp = remote(OS.at[there], out.at[row], osend.at[o - 1], orecv.at[o - 1], (tm, there, col))
-        cp.start()
-        out_copies.append(cp)
-    own_out = local(OS.at[row], out.at[row], loc_sem.at[6])
+    own_out = pltpu.make_async_copy(OS.at[row], out.at[row], loc_sem.at[6])
+
+    def send_tile(rr):
+        o = lax.rem(rr - row + nrow, nrow)
+
+        @pl.when(row != rr)
+        def _():
+            remote(OS.at[rr], out.at[row], osend.at[o - 1], orecv.at[o - 1], (tm, rr, col)).start()
+
+        @pl.when(row == rr)
+        def _():
+            own_out.start()
+
+    out_copies = [
+        remote(
+            OS.at[lax.rem(row + o, nrow)],
+            out.at[row],
+            osend.at[o - 1],
+            orecv.at[o - 1],
+            (tm, lax.rem(row + o, nrow), col),
+        )
+        for o in range(1, nrow)
+    ]
+    for parts, tiles in PLAN:
+        for p in parts:
+            dilated(p, 0)
+        for p in parts:
+            taps(p, 0)
+        for p in tiles:
+            head(p, 0)
+        for p in tiles:
+            send_tile(p)
     own_out.wait()
     for cp in out_copies:
         cp.wait_recv()

time: 30.3 us -> 29.5 us (0.974)
  the two profiles are of different devices: /device:TPU:224 before, /device:TPU:232 now
where the time goes in v6:
time: 29.5 us; the launch traced here: 29.3 us
  Pallas kernels  28 us (95%)
  local copies, waits for them, and re-layouts  1.32 us (4%)
    pallas_call x1, Pallas kernels, step(): pl.pallas_call(functools.partial(kernel, ntm, ncol), out_shape=jax.ShapeD...  28 us
    unnamed x1, local copies, waits for them, and re-layouts  1.32 us

profile of v6, /device:TPU:232, one launch (start us, length us, event | category | flops | bytes accessed | tf_op | source)
XLA Modules:
  0.0 29.3 jit_solution(17732586525000852724)
XLA Ops:
  0.0 28.0 %shard_map.73 = f32[4,2,4,128]{3,2,1,0:T(4,128)} custom-call(s32[4]{0:T(128)} %bitcast.5, bf16[4,4,128,128]{3,2,1,0:T(8,128)(2,1)} %feat.1, bf16[1,4,128,128]{3,2,1,0:T(8,128)(2,1)} %keys.1, bf16[81,128]{1,0:T(8,128)(2,1)} %mw.1, bf16[3,3,256,128]{3,2,1,0:T(8,128)(2,1)} %jw.1, bf16[3,384,128]{2,1,0:T(8,128)(2,1)} %bitcast.3, bf16[2,1152]{1,0:T(2,128)(2,1)} %bitcast.4), custom_call_target="tpu_custom_call" | custom-call | tf_op jit(solution)/shard_map/pallas_call | solution.py:585
  28.0 1.3 %copy.11 = f32[4,2,4,128]{3,2,1,0:T(4,128)} copy(f32[4,2,4,128]{3,2,1,0:T(4,128)} %shard_map.73) | data formatting | bytes 32768
